TPU v7x, 32 devices: a whole 2x2x4 slice. The times are simulated.
32 devices in a mesh: groups: 2 (over y), seq: 8 (over z, x), head: 1, sub: 2 (over core).
Axes of the slice: x: 2, y: 2, z: 4, core: 2. Of those that a mesh axis runs over, the one named last changes fastest.
Arguments:
- queries: bfloat16 [8, 32768, 512], P('head', ('groups', 'seq', 'sub')), parts along dimension 1, may hold values from -6 to 6
- keys: bfloat16 [8, 32768, 512], P('head', ('groups', 'seq', 'sub')), parts along dimension 1, may hold values from -6 to 6
- values: bfloat16 [8, 32768, 512], P('head', ('groups', 'seq', 'sub')), parts along dimension 1, may hold values from -6 to 6
- lr_codes: int32 [8, 32768], P('head', ('groups', 'seq', 'sub')), parts along dimension 1, may hold values from 0 to 15
- fast_gate: float32 [8, 512, 512], P('head', ('seq', 'sub')), may hold values from -0.25 to 0.25
- fast_up: float32 [8, 512, 512], P('head', ('seq', 'sub')), may hold values from -0.25 to 0.25
- fast_down: float32 [8, 512, 512], P('head', ('seq', 'sub')), may hold values from -0.25 to 0.25
Outputs:
- fast_out: bfloat16 [8, 32768, 512], P('head', ('groups', 'seq', 'sub')), parts along dimension 1
There are 2 independent parts, one for each index of `groups`. A program takes and returns all parts, laid end to end along the dimension named above; an argument that names none is the same for every part. Nothing has to cross between parts.
All inputs are finite; a program needn't handle non-finite values.
Results may differ from a plain program's by a relative error of at most 0.0085.
Values may be sent and summed in bfloat16 or wider, within the bound.
No kernel may reach another device: no remote copies, remote signals or barrier semaphores. Data moves between devices by JAX's collectives and lax.ppermute only.
A program may use at most 192 MiB of HBM per device.

v0:
```python
import functools

import jax
import jax.numpy as jnp
from jax import lax
from jax.experimental import pallas as pl
from jax.experimental.pallas import tpu as pltpu
from jax.sharding import PartitionSpec as P

EPSILON = 1e-06
STEP_SIZE = 0.5
BF16 = jnp.bfloat16
F32 = jnp.float32
VMEM_LIMIT = 64 * 1024 * 1024


def column_squares(matrix):
    return jnp.sum(matrix * matrix, axis=1)


def rescale(moved, col_weight, col_moved):
    return moved * jnp.sqrt((col_weight + EPSILON) / (col_moved + EPSILON))[:, None, :]


def step_scale(col_weight, grad_total):
    return (
        STEP_SIZE * jnp.sqrt(jnp.sum(col_weight, axis=1) + EPSILON) / jnp.sqrt(grad_total + EPSILON)
    )


def apply_fast(queries, gate_b, up_b, down_b):
    query_gate = jnp.einsum("htd,hdf->htf", queries, gate_b, preferred_element_type=jnp.float32)
    query_up = jnp.einsum("htd,hdf->htf", queries, up_b, preferred_element_type=jnp.float32)
    query_hidden = (jax.nn.silu(query_gate) * query_up).astype(jnp.bfloat16)
    return jnp.einsum(
        "htf,hfd->htd", query_hidden, down_b, preferred_element_type=jnp.float32
    ).astype(jnp.bfloat16)


def local_grads(keys, target, gate_b, up_b, down_b):
    gate_pre = jnp.einsum("htd,hdf->htf", keys, gate_b, preferred_element_type=jnp.float32)
    up_pre = jnp.einsum("htd,hdf->htf", keys, up_b, preferred_element_type=jnp.float32)
    sigmoid_gate = jax.nn.sigmoid(gate_pre)
    hidden = (gate_pre * sigmoid_gate * up_pre).astype(jnp.bfloat16)
    back = jnp.einsum("htd,hfd->htf", target, down_b, preferred_element_type=jnp.float32)
    grad_gate_pre = (back * up_pre * sigmoid_gate * (1.0 + gate_pre * (1.0 - sigmoid_gate))).astype(
        jnp.bfloat16
    )
    grad_up_pre = (back * gate_pre * sigmoid_gate).astype(jnp.bfloat16)
    grad_gate = jnp.einsum("htd,htf->hdf", keys, grad_gate_pre, preferred_element_type=jnp.float32)
    grad_up = jnp.einsum("htd,htf->hdf", keys, grad_up_pre, preferred_element_type=jnp.float32)
    grad_down = jnp.einsum("htf,htd->hfd", hidden, target, preferred_element_type=jnp.float32)
    return (grad_gate, grad_up, grad_down)


def on_device_generic(queries, keys, values, lr_codes, fast_gate, fast_up, fast_down):
    token_rates = (lr_codes.astype(jnp.float32) + 1.0) / 16.0
    target = (-token_rates[:, :, None] * values.astype(jnp.float32)).astype(jnp.bfloat16)
    gate_b, up_b, down_b = (
        lax.all_gather(fast_gate.astype(jnp.bfloat16), ("seq", "sub"), axis=1, tiled=True),
        lax.all_gather(fast_up.astype(jnp.bfloat16), ("seq", "sub"), axis=1, tiled=True),
        lax.all_gather(fast_down.astype(jnp.bfloat16), ("seq", "sub"), axis=1, tiled=True),
    )
    grad_gate, grad_up, grad_down = local_grads(keys, target, gate_b, up_b, down_b)
    owned = (
        lax.psum_scatter(grad_gate, ("seq", "sub"), scatter_dimension=1, tiled=True),
        lax.psum_scatter(grad_up, ("seq", "sub"), scatter_dimension=1, tiled=True),
        lax.psum_scatter(grad_down, ("seq", "sub"), scatter_dimension=1, tiled=True),
    )
    weights = (fast_gate, fast_up, fast_down)
    grad_local = jnp.stack(
        [
            jnp.sum(owned[0] * owned[0], axis=(1, 2)),
            jnp.sum(owned[1] * owned[1], axis=(1, 2)),
            jnp.sum(owned[2] * owned[2], axis=(1, 2)),
        ],
        axis=1,
    )
    col_gate, col_up, col_down, grad_totals = lax.psum(
        (column_squares(fast_gate), column_squares(fast_up), column_squares(fast_down), grad_local),
        ("seq", "sub"),
    )
    col_weights = (col_gate, col_up, col_down)
    moved_all = []
    for index in range(3):
        scale = step_scale(col_weights[index], grad_totals[:, index])
        moved_all.append(weights[index] - scale[:, None, None] * owned[index])
    moved_cols = lax.psum(
        (column_squares(moved_all[0]), column_squares(moved_all[1]), column_squares(moved_all[2])),
        ("seq", "sub"),
    )
    renewed = [
        rescale(moved_all[index], col_weights[index], moved_cols[index]).astype(jnp.bfloat16)
        for index in range(3)
    ]
    new_gate, new_up, new_down = (
        lax.all_gather(renewed[0], ("seq", "sub"), axis=1, tiled=True),
        lax.all_gather(renewed[1], ("seq", "sub"), axis=1, tiled=True),
        lax.all_gather(renewed[2], ("seq", "sub"), axis=1, tiled=True),
    )
    return apply_fast(queries, new_gate, new_up, new_down)


def block(shape, index_map):
    return pl.BlockSpec(shape, index_map)


def whole(array):
    return pl.BlockSpec(array.shape, lambda *_: (0,) * array.ndim)


def anywhere():
    return pl.BlockSpec(memory_space=pl.ANY)


def call(body, name, positions, grid, operands, in_specs, out_shapes, out_specs, scratch=(), aliases=None, estimate=None, vmem=VMEM_LIMIT):
    return pl.pallas_call(
        body,
        name=name,
        out_shape=out_shapes,
        grid_spec=pltpu.PrefetchScalarGridSpec(
            num_scalar_prefetch=1,
            grid=grid,
            in_specs=in_specs,
            out_specs=out_specs,
            scratch_shapes=list(scratch),
        ),
        input_output_aliases=aliases or {},
        compiler_params=pltpu.CompilerParams(vmem_limit_bytes=vmem),
        cost_estimate=estimate,
    )(positions, *operands)


def sds(shape, dtype):
    return jax.ShapeDtypeStruct(shape, dtype)


def cost(microseconds):
    return pl.CostEstimate(flops=0, bytes_accessed=int(microseconds * 3e6), transcendentals=0)


def first_pieces(positions, own, received, k, after):
    heads, rows, columns = own[0].shape
    half, width = heads // 2, columns // 2

    def body(pos, *refs):
        mine = pl.ds(pl.multiple_of(pos[0] * rows, rows), rows)
        theirs = pl.ds(pl.multiple_of((1 - pos[0]) * rows, rows), rows)
        everything, sends = refs[-half - 1], refs[-half:]
        for head in range(half):
            for m in range(3):
                everything[head, m, mine, :] = refs[m][head].astype(BF16)
                everything[head, m, theirs, :] = refs[3 + m][head].astype(BF16)
        for j, out_ref in enumerate(sends):
            out_ref[...] = everything[pos[1] ^ (j ^ k)]

    spec = block((half, rows, width), lambda i, pos: (pos[0], 0, pos[3]))
    outs = [sds((half, 3, 2 * rows, width), BF16)] + [sds((3, 2 * rows, width), BF16)] * half
    return call(
        body, "first_pieces", positions, (1,), (*own, *received, *after),
        [spec] * 6 + [anywhere()] * len(after), outs, [whole(o) for o in outs], vmem=60 * 1024 * 1024,
    )


def next_pieces(positions, arrived, rows, k, after, handed=None):
    half = len(arrived)
    more = [] if k is None else list(rows)

    passed = [] if handed is None else [handed]

    def body(pos, *refs):
        held, *sends = refs[half + len(more) + len(after) + len(passed) :]
        for j in range(half):
            held[j] = refs[j][...]
        if more:
            height = rows[0].shape[2]
            for ref, x in ((refs[half], pos[2]), (refs[half + 1], 1 - pos[2])):
                at = pl.ds(pl.multiple_of(x * height, height), height)
                for j in range(half):
                    sends[j][:, at, :] = ref[pos[1] ^ (j ^ k)]

    outs = [sds((half, *arrived[0].shape), BF16)]
    if more:
        outs += [sds((3, 2 * rows[0].shape[2], rows[0].shape[3]), BF16)] * half
    operands = (*arrived, *more)
    others = (*after, *passed)
    aliases = {len(operands) + len(others): len(outs)} if passed else {}
    return call(
        body, "next_pieces", positions, (1,), (*operands, *others),
        [whole(a) for a in operands] + [anywhere()] * len(others),
        outs + [sds(p.shape, p.dtype) for p in passed], [whole(o) for o in outs] + [anywhere() for _ in passed],
        aliases=aliases, estimate=cost(3),
    )


def copied(positions, array, after):
    def body(pos, in_ref, *rest):
        rest[-1][...] = in_ref[...]

    shape = sds(array.shape, BF16)
    return call(body, "copied", positions, (1,), (array, *after), [whole(array)] + [anywhere()] * len(after), shape, whole(shape))


def token_rates(positions, codes, half, after):
    tokens = codes[0].shape[1]

    def body(pos, *refs):
        head = pos[0] * half + pl.program_id(0)
        for ref, out_ref in zip(refs, refs[-2:]):
            row = (ref[pl.ds(head, 1), :].astype(F32) + 1.0) / 16.0
            out_ref[0] = jnp.broadcast_to(row, (128, tokens)).T.astype(BF16)

    shape = sds((half, tokens, 128), BF16)
    out = block((1, tokens, 128), lambda i, pos: (i, 0, 0))
    return call(
        body, "token_rates", positions, (half,), (*codes, *after), [whole(c) for c in codes] + [anywhere()] * len(after),
        [shape] * 2, [out] * 2,
    )


def other_half(positions, array, half, after):
    def body(pos, in_ref, *rest):
        rest[-1][...] = in_ref[...]

    _, tokens, columns = array.shape
    spec = block((1, tokens // 2, columns), lambda i, j, pos: ((1 - pos[0]) * half + i, j, 0))
    out = block((1, tokens // 2, columns), lambda i, j, pos: (i, j, 0))
    return call(
        body, "other_half", positions, (half, 2), (array, *after), [spec] + [anywhere()] * len(after),
        sds((half, tokens, columns), BF16), out, estimate=cost(3),
    )


def gradients(positions, keys, values, rates, pieces, k, half, after, cuts):
    z_size, _, piece_rows, width = pieces[0].shape
    tokens, columns = keys[0].shape[1:]
    lanes = rates[0].shape[2]
    rows = columns
    quarter = rows // z_size
    tile = tokens // 2 if tokens % 32 == 0 else tokens
    chunks = 2 * tokens // tile
    last = k == 0
    n_in = 6 + len(pieces) + len(after)

    def body(pos, *refs):
        streams, parts = (refs[0:2], refs[2:4], refs[4:6]), refs[6 : 6 + len(pieces)]
        keep, sends = refs[n_in], refs[n_in + 1 : n_in + 1 + cuts]
        w, key, value, rate, grads, hidden, target, total, rounded, sems_w, sems_in, sems_out = refs[-12:]
        z, x, y = pos[1], pos[2], pos[3]
        mine = pl.ds(pl.multiple_of(x * width, 128), width)
        theirs = pl.ds(pl.multiple_of((1 - x) * width, 128), width)

        places = ((0, y), (0, 1 - y)) if len(parts) == 2 else ((x, y), (1 - x, y), (x, 1 - y), (1 - x, 1 - y))
        weight_copies = []
        for n, (ref, (xx, yy)) in enumerate(zip(parts, places)):
            cols = pl.ds(pl.multiple_of(yy * width, 128), width)
            for j in range(z_size):
                at = pl.ds(pl.multiple_of((z ^ j) * quarter + xx * piece_rows, piece_rows), piece_rows)
                weight_copies.append(pltpu.make_async_copy(ref.at[j], w.at[:, at, cols], sems_w.at[n, j]))
        token_copies = []
        heads = (pos[0] * half + (z ^ k),) * 2 + (z ^ k,)
        for c in range(chunks):
            source, first = divmod(c * tile, tokens)
            here = pl.ds(c * tile, tile)
            there = pl.ds(first, tile)
            token_copies.append([
                pltpu.make_async_copy(pair[source].at[head, there], buffer.at[here], sems_in.at[n, c])
                for n, (pair, head, buffer) in enumerate(zip(streams, heads, (key, value, rate)))
            ])
        for copy in weight_copies + [copy for group in token_copies for copy in group]:
            copy.start()
        for copy in weight_copies:
            copy.wait()

        def own_copy():
            return pltpu.make_async_copy(w.at[:, :, mine], refs[n_in + 1 + cuts], sems_out.at[3, 0])

        def out_copies(m):
            copies = [pltpu.make_async_copy(total.at[m, :, mine], keep.at[m], sems_out.at[m, cuts])]
            for n in range(cuts):
                cut = pl.ds(n * (rows // cuts), rows // cuts)
                copies.append(pltpu.make_async_copy(rounded.at[m, cut], sends[n].at[m], sems_out.at[m, n]))
            return copies

        if last:
            own_copy().start()
            squares = refs[n_in + 2 + cuts]
            for m in range(3):
                full = w[m].astype(F32)
                squares[m : m + 1, :] = jnp.sum(full * full, axis=0, keepdims=True)

        @pl.loop(0, chunks)
        def _(c):
            here = pl.ds(pl.multiple_of(c * tile, tile), tile)
            for n, (pair, head, buffer) in enumerate(zip(streams, heads, (key, value, rate))):
                pltpu.make_async_copy(pair[0].at[head, pl.ds(0, tile)], buffer.at[here], sems_in.at[n, c]).wait()
            tokens_rate = jnp.concatenate([rate[here, :].astype(F32)] * (columns // lanes), axis=1)
            t = (-tokens_rate * value[here, :].astype(F32)).astype(BF16)
            target[here, :] = t
            gate = jnp.dot(key[here, :], w[0], preferred_element_type=F32)
            up = jnp.dot(key[here, :], w[1], preferred_element_type=F32)
            back = lax.dot_general(t, w[2], (((1,), (1,)), ((), ())), preferred_element_type=F32)
            sig = 0.5 * jnp.tanh(0.5 * gate) + 0.5
            silu = gate * sig
            hidden[here, :] = (silu * up).astype(BF16)
            grads[1, here, :] = (back * silu).astype(BF16)
            grads[0, here, :] = (back * up * (sig + silu * (1.0 - sig))).astype(BF16)

        def product(m, a, b):
            total[m] = lax.dot_general(a, b, (((0,), (0,)), ((), ())), preferred_element_type=F32)
            rounded[m] = total[m, :, theirs].astype(BF16)
            for copy in out_copies(m):
                copy.start()

        @pl.loop(0, 2)
        def _(m):
            product(m, key[...], grads[m])

        product(2, hidden[...], target[...])
        for m in range(3):
            for copy in out_copies(m):
                copy.wait()
        if last:
            own_copy().wait()

    outs = [sds((3, rows, width), F32)] + [sds((3, rows // cuts, width), BF16)] * cuts
    out_specs = [anywhere()] * len(outs)
    if last:
        outs += [sds((3, rows, width), BF16), sds((8, columns), F32)]
        out_specs += [anywhere(), whole(outs[-1])]
    operands = (*keys, *values, *rates, *pieces, *after)
    bf16_rows = pltpu.VMEM((2 * tokens, columns), BF16)
    return call(
        body, "gradients", positions, (1,), operands, [anywhere()] * len(operands), outs, out_specs,
        [
            pltpu.VMEM((3, rows, columns), BF16), bf16_rows, bf16_rows, pltpu.VMEM((2 * tokens, lanes), BF16),
            pltpu.VMEM((2, 2 * tokens, columns), BF16), bf16_rows, bf16_rows,
            pltpu.VMEM((3, rows, columns), F32), pltpu.VMEM((3, rows, width), BF16),
            pltpu.SemaphoreType.DMA((len(pieces), z_size)), pltpu.SemaphoreType.DMA((3, chunks)), pltpu.SemaphoreType.DMA((4, cuts + 1)),
        ],
        estimate=pl.CostEstimate(flops=6 * 2 * 2 * tokens * rows * columns, bytes_accessed=14 * 2**20, transcendentals=2 * tokens * columns),
    )


def added(positions, keep, received, after, dtype=BF16, microseconds=1, cuts=1):
    rows = keep.shape[1]

    def body(pos, keep_ref, *refs):
        for m in range(3):
            for c in range(cuts):
                at = pl.ds(c * (rows // cuts), rows // cuts)
                total = keep_ref[m, at, :] + refs[c][m].astype(F32)
                for ref in refs[cuts : len(received)]:
                    total = total + ref[m, at, :].astype(F32)
                refs[-1][m, at, :] = total.astype(dtype)

    operands = (keep, *received)
    shape = sds(keep.shape, dtype)
    specs = [whole(a) for a in operands] + [anywhere()] * len(after)
    return call(body, "added", positions, (1,), (*operands, *after), specs, shape, whole(shape), estimate=cost(microseconds))


def total_gradient(positions, keep, received):
    def body(pos, keep_ref, *refs):
        grad, sums = refs[-2:]
        sums[...] = jnp.zeros_like(sums)
        for m in range(3):
            total = keep_ref[m]
            for ref in refs[:-2]:
                total = total + ref[m].astype(F32)
            grad[m] = total
            columns = jnp.sum(total * total, axis=0, keepdims=True)
            sums[m : m + 1, :] = jnp.broadcast_to(jnp.sum(columns, axis=1, keepdims=True), (1, sums.shape[1]))

    outs = [sds(keep.shape, F32), sds((8, 128), F32)]
    operands = (keep, *received)
    return call(body, "total_gradient", positions, (1,), operands, [whole(a) for a in operands], outs, [whole(o) for o in outs])


def renewed_block(positions, grad, own_w, squares, sums, sums_in):
    width = grad.shape[2]

    def body(pos, g_ref, w_ref, sq_ref, sums_ref, sums_in_ref, out):
        mine = pl.ds(pl.multiple_of(pos[2] * width, 128), width)
        for m in range(3):
            total_g = sums_ref[m : m + 1, :1] + sums_in_ref[m : m + 1, :1]
            total_w = jnp.sum(sq_ref[m : m + 1, :], axis=1, keepdims=True)
            scale = STEP_SIZE * jnp.sqrt(total_w + EPSILON) / jnp.sqrt(total_g + EPSILON)
            moved = w_ref[m].astype(F32) - scale * g_ref[m]
            col_moved = jnp.sum(moved * moved, axis=0, keepdims=True)
            out[m] = (moved * jnp.sqrt((sq_ref[m : m + 1, mine] + EPSILON) / (col_moved + EPSILON))).astype(BF16)

    operands = (grad, own_w, squares, sums, sums_in)
    shape = sds(grad.shape, BF16)
    return call(body, "renewed_block", positions, (1,), operands, [whole(a) for a in operands], shape, whole(shape))


def apply_renewed(positions, queries, queries_in, held, swapped, k, half, out, late, after):
    _, rows, width = held.shape
    columns = 2 * width
    heads, tokens, _ = queries.shape
    tile = tokens // 2 if tokens % 32 == 0 else tokens
    chunks = 2 * tokens // tile
    blocks = [b for _, b in late]
    n_in = 4 + len(blocks) + len(after) + (0 if out is None else 1)

    def body(pos, q0, q1, held_ref, swapped_ref, *refs):
        late_refs = refs[: len(blocks)]
        out_ref, send_ref, w, query, result, brought, sems_in, sems_q, sems_out, sems_late = refs[n_in - 4 :]
        x = pos[2]
        heads_of = (pos[0] * half + (pos[1] ^ k), pos[1] ^ k)
        weights = [
            pltpu.make_async_copy(ref, w.at[:, :, pl.ds(pl.multiple_of(xx * width, 128), width)], sems_in.at[n])
            for n, (ref, xx) in enumerate(((held_ref, x), (swapped_ref, 1 - x)))
        ]
        loads, stores = [], []
        for c in range(chunks):
            source, first = divmod(c * tile, tokens)
            here, there = pl.ds(c * tile, tile), pl.ds(first, tile)
            loads.append(pltpu.make_async_copy((q0, q1)[source].at[heads_of[source], there], query.at[here], sems_q.at[c]))
            to = send_ref.at[there] if source else out_ref.at[heads_of[0], there]
            stores.append(pltpu.make_async_copy(result.at[here], to, sems_out.at[c]))
        late_in = [pltpu.make_async_copy(ref, brought.at[n], sems_late.at[n, 0]) for n, ref in enumerate(late_refs)]
        late_out = [
            pltpu.make_async_copy(brought.at[n], out_ref.at[(1 - pos[0]) * half + (pos[1] ^ late[n][0])], sems_late.at[n, 1])
            for n in range(len(blocks))
        ]
        for copy in weights + loads + late_in:
            copy.start()
        for copy in weights:
            copy.wait()

        @pl.loop(0, chunks)
        def _(c):
            here = pl.ds(pl.multiple_of(c * tile, tile), tile)
            there = pl.ds(pl.multiple_of(lax.rem(c * tile, tokens), tile), tile)
            pltpu.make_async_copy(q1.at[heads_of[1], pl.ds(0, tile)], query.at[here], sems_q.at[c]).wait()
            q = query[here, :]
            gate = jnp.dot(q, w[0], preferred_element_type=F32)
            up = jnp.dot(q, w[1], preferred_element_type=F32)
            hidden = (gate * (0.5 * jnp.tanh(0.5 * gate) + 0.5) * up).astype(BF16)
            result[here, :] = jnp.dot(hidden, w[2], preferred_element_type=F32).astype(BF16)

            @pl.when(c < chunks // 2)
            def _():
                pltpu.make_async_copy(result.at[here], out_ref.at[heads_of[0], there], sems_out.at[c]).start()

            @pl.when(c >= chunks // 2)
            def _():
                pltpu.make_async_copy(result.at[here], send_ref.at[there], sems_out.at[c]).start()

            @pl.when(c == 0)
            def _():
                for n in range(len(blocks)):
                    late_in[n].wait()
                    late_out[n].start()

        for copy in stores + late_out:
            copy.wait()

    operands = [queries, queries_in, held, swapped, *blocks, *after]
    aliases = {}
    if out is not None:
        aliases = {1 + len(operands): 0}
        operands.append(out)
    return call(
        body, "apply_renewed", positions, (1,), operands, [anywhere()] * len(operands),
        [sds(queries.shape, BF16), sds((tokens, columns), BF16)], [anywhere()] * 2,
        [
            pltpu.VMEM((3, rows, columns), BF16), pltpu.VMEM((2 * tokens, columns), BF16), pltpu.VMEM((2 * tokens, columns), BF16),
            pltpu.VMEM((max(len(blocks), 1), tokens, columns), BF16),
            pltpu.SemaphoreType.DMA((2,)), pltpu.SemaphoreType.DMA((chunks,)), pltpu.SemaphoreType.DMA((chunks,)),
            pltpu.SemaphoreType.DMA((max(len(blocks), 1), 2)),
        ],
        aliases,
        pl.CostEstimate(flops=3 * 2 * 2 * tokens * rows * columns, bytes_accessed=7 * 2**20, transcendentals=2 * tokens * columns),
    )


def place(positions, out, late, half):
    n = len(late)
    tokens, columns = late[0][1].shape
    cuts = 4 if tokens % 64 == 0 else 1
    tile = tokens // cuts

    def body(pos, *refs):
        out_ref, held, sems_in, sems_out = refs[-4:]
        pairs = []
        for i, (k, _) in enumerate(late):
            head = (1 - pos[0]) * half + (pos[1] ^ k)
            for c in range(cuts):
                at = pl.ds(c * tile, tile)
                pairs.append((
                    pltpu.make_async_copy(refs[i].at[at], held.at[i, at], sems_in.at[i, c]),
                    pltpu.make_async_copy(held.at[i, at], out_ref.at[head, at], sems_out.at[i, c]),
                ))
        for first, _ in pairs:
            first.start()
        for first, second in pairs:
            first.wait()
            second.start()
        for _, second in pairs:
            second.wait()

    return call(
        body, "place", positions, (1,), (*(b for _, b in late), out), [anywhere()] * (n + 1),
        sds(out.shape, BF16), anywhere(),
        [pltpu.VMEM((n, tokens, columns), BF16), pltpu.SemaphoreType.DMA((n, cuts)), pltpu.SemaphoreType.DMA((n, cuts))],
        {1 + n: 0}, cost(1),
    )


def on_device_fast(queries, keys, values, lr_codes, fast_gate, fast_up, fast_down):
    heads, tokens, _ = queries.shape
    half = heads // 2
    core, seq = lax.axis_index("sub"), lax.axis_index("seq")
    positions = jnp.stack([core, seq // 2, seq % 2, lax.axis_index("groups")]).astype(jnp.int32)
    flip = [(0, 1), (1, 0)]

    def over_sub(a):
        return lax.ppermute(a, "sub", flip)

    def over_groups(a):
        return lax.ppermute(a, "groups", flip)

    def over_x(a):
        return lax.ppermute(a, "seq", [(i, i ^ 1) for i in range(8)])

    def over_z(a, j):
        return lax.ppermute(a, "seq", [(i, i ^ (2 * j)) for i in range(8)])

    weights = (fast_gate, fast_up, fast_down)
    rows_in = tuple(over_sub(w) for w in weights)
    all_keys, all_values = (keys, over_sub(keys)), (values, over_sub(values))
    codes = (lr_codes, over_sub(lr_codes))

    def head_gradients(k, pieces, after):
        keep, send, *rest = gradients(positions, all_keys, all_values, rates, pieces, k, half, after, 1)
        return keep, over_x(send), *rest

    def turn(pieces, k, after, handed=None):
        arrived = (pieces[0], *(over_z(a, j) for j, a in enumerate(pieces[1:], 1)))
        return next_pieces(positions, arrived, rows, k, after, handed)

    everything, *pieces = first_pieces(positions, weights, rows_in, 3, ())
    rows = (everything, over_x(everything))
    held, *pieces = turn(pieces, 2, ())
    swapped = over_x(held)
    pieces3 = (held, swapped, over_groups(held), over_groups(swapped))
    rates = token_rates(positions, codes, half, (held,))
    queries_in = over_sub(other_half(positions, queries, half, (held,)))
    held, *pieces = turn(pieces, 1, (*pieces3, *rates))
    pieces2 = (held, over_groups(held))
    keep3, *sends = gradients(positions, all_keys, all_values, rates, pieces3, 3, half, (held,), 4)
    held, *pieces = turn(pieces, 0, (keep3, pieces2[1]))
    pieces1 = (held, over_groups(held))
    keep2, send2 = gradients(positions, all_keys, all_values, rates, pieces2, 2, half, (held,), 1)
    in3 = [over_x(a) for a in sends]
    sum3 = added(positions, keep3, in3, (keep2,), cuts=4)
    from1 = over_z(sum3, 1)
    (held,) = turn(pieces, None, (sum3, pieces1[1]))
    pieces0 = (held, over_groups(held))
    keep1, send1 = gradients(positions, all_keys, all_values, rates, pieces1, 1, half, (held,), 1)
    in2 = over_x(send2)
    sum2 = added(positions, keep2, (in2, from1), (keep1,))
    from2 = over_z(sum2, 2)
    keep0, in0, own_w, squares = head_gradients(0, pieces0, (sum2,))
    in1 = over_x(send1)
    sum1 = added(positions, keep1, (in1,), (keep0,))
    from1 = over_z(sum1, 1)
    partial = added(positions, keep0, (from2,), (sum1,), F32, 8)
    grad, sums = total_gradient(positions, partial, (in0, from1))
    renewed = renewed_block(positions, grad, own_w, squares, sums, over_x(sums))

    swapped = over_x(renewed)
    from1, from2 = over_z(renewed, 1), over_z(renewed, 2)
    from3 = over_z(from2, 1)
    matrices = {0: (renewed, swapped), 2: (from2, over_x(from2)), 3: (from3, over_x(from3))}

    def head_output(k, out, late, after):
        out, sent = apply_renewed(positions, queries, queries_in, *matrices[k], k, half, out, late, after)
        return out, (k, over_sub(sent))

    out, late0 = head_output(0, None, (), (from1, from2))
    swapped_late = copied(positions, swapped, (from3, out))
    matrices[1] = (from1, over_z(swapped_late, 1))
    out, late2 = head_output(2, out, (), (swapped_late,))
    out, late1 = head_output(1, out, (late0,), matrices[3])
    out, late3 = head_output(3, out, (late2,), ())
    return place(positions, out, (late1, late3), half)


def solution(mesh):
    seq, sub, groups = mesh.shape["seq"], mesh.shape["sub"], mesh.shape["groups"]

    def on_device(queries, *rest):
        rows, columns = rest[3].shape[1:]
        fits = (groups, seq, sub, queries.shape[0]) == (2, 8, 2, 8) and rows % 32 == 0 and columns == seq * sub * rows and columns % 256 == 0
        return (on_device_fast if fits else on_device_generic)(queries, *rest)

    return jax.shard_map(
        on_device,
        mesh=mesh,
        in_specs=(
            P("head", ("groups", "seq", "sub"), None),
            P("head", ("groups", "seq", "sub"), None),
            P("head", ("groups", "seq", "sub"), None),
            P("head", ("groups", "seq", "sub")),
            P("head", ("seq", "sub"), None),
            P("head", ("seq", "sub"), None),
            P("head", ("seq", "sub"), None),
        ),
        out_specs=P("head", ("groups", "seq", "sub"), None),
        check_vma=False,
    )
```

profile of v0, /device:TPU:0, one launch (start us, length us, event | category | flops | bytes accessed | tf_op | source)
XLA Modules:
  0.0 299.3 jit_solution(17470854354273632112)
XLA Ops:
  2.1 6.0 %collective-permute-done.refs_3_ = f32[8,32,512]{2,1,0:T(8,128)S(1)} collective-permute-done((f32[8,32,512]{2,1,0:T(8,128)}, f32[8,32,512]{2,1,0:T(8,128)S(1)}, u32[]{:S(2)}, u32[]{:S(2)}) %collective-permute-start) | collective-permute-done | bytes 524320 | tf_op jit(solution)/shard_map/ppermute | solution.py:521
  22.5 4.7 %collective-permute-start.5 = (bf16[3,64,256]{2,1,0:T(8,128)(2,1)}, bf16[3,64,256]{2,1,0:T(8,128)(2,1)}, u32[]{:S(2)}, u32[]{:S(2)}) collective-permute-start(bf16[3,64,256]{2,1,0:T(8,128)(2,1)} %get-tuple-element.53), channel_id=1, source_target_pairs={{0,12},{2,14},{4,8},{6,10},{8,4},{10,6},{12,0},{14,2},{1,13},{3,15... | collective-permute-start | bytes 294920 | tf_op jit(solution)/shard_map/ppermute | solution.py:530
  43.3 5.9 %collective-permute-done.12.refs_2_ = bf16[3,128,256]{2,1,0:T(8,128)(2,1)} collective-permute-done((bf16[3,128,256]{2,1,0:T(8,128)(2,1)}, bf16[3,128,256]{2,1,0:T(8,128)(2,1)}, u32[]{:S(2)}, u32[]{:S(2)}) %collective-permute-start.12) | collective-permute-done | bytes 196640 | tf_op jit(solution)/shard_map/ppermute | solution.py:530
  51.5 3.6 %token_rates.1 = (bf16[4,1024,128]{2,1,0:T(8,128)(2,1)}, bf16[4,1024,128]{2,1,0:T(8,128)(2,1)}) custom-call(s32[4]{0:T(128)} %pad_add_fusion.pos, s32[8,1024]{1,0:T(8,128)} %refs_0_.7, s32[8,1024]{1,0:T(8,128)} %collective-permute-done.10.refs_1_, bf16[4,3,64,256]{3,2,1,0:T(8,128)(2,1)} %get-tuple-element.55.rest_0_.refs_2_.refs_6_), custom_call_target="tpu_custom_call" | custom-call | tf_op jit(solution)/shard_map/token_rates/pallas_call | solution.py:117
  68.5 12.0 %gradients.4 = (f32[3,512,256]{2,1,0:T(8,128)}, bf16[3,128,256]{2,1,0:T(8,128)(2,1)}, bf16[3,128,256]{2,1,0:T(8,128)(2,1)}, bf16[3,128,256]{2,1,0:T(8,128)(2,1)}, bf16[3,128,256]{2,1,0:T(8,128)(2,1)}) custom-call(s32[4]{0:T(128)} %pad_add_fusion.pos, bf16[8,1024,512]{2,1,0:T(8,128)(2,1)} %refs_0_.11, bf16[8,1024,512]{2,1,0:T(8,128)(2,1)} %collective-permute-done.8.refs_1_, ...), custom_call_target="tpu_custom_call" | custom-call | flops 6442450944 | bytes 14680064 | tf_op jit(solution)/shard_map/gradients/pallas_call | solution.py:117
  84.6 3.4 %next_pieces.6 = (bf16[4,3,128,256]{3,2,1,0:T(8,128)(2,1)}, bf16[3,128,256]{2,1,0:T(8,128)(2,1)}, bf16[3,128,256]{2,1,0:T(8,128)(2,1)}, bf16[3,128,256]{2,1,0:T(8,128)(2,1)}, bf16[3,128,256]{2,1,0:T(8,128)(2,1)}) custom-call(s32[4]{0:T(128)} %pad_add_fusion.pos, bf16[3,128,256]{2,1,0:T(8,128)(2,1)} %get-tuple-element.62.refs_0_, ...), custom_call_target="tpu_custom_call" | custom-call | bytes 9000000 | tf_op jit(solution)/shard_map/next_pieces/pallas_call | solution.py:117
  88.4 7.3 %other_half.1 = bf16[4,1024,512]{2,1,0:T(8,128)(2,1)} custom-call(s32[4]{0:T(128)} %pad_add_fusion.pos, bf16[8,1024,512]{2,1,0:T(8,128)(2,1)} %q0.7, bf16[4,3,64,256]{3,2,1,0:T(8,128)(2,1)} %get-tuple-element.55.rest_0_.refs_2_.refs_6_), custom_call_target="tpu_custom_call" | custom-call | bytes 9000000 | tf_op jit(solution)/shard_map/other_half/pallas_call | solution.py:117
  100.2 11.8 %gradients.5 = (f32[3,512,256]{2,1,0:T(8,128)}, bf16[3,512,256]{2,1,0:T(8,128)(2,1)}) custom-call(s32[4]{0:T(128)} %pad_add_fusion.pos, bf16[8,1024,512]{2,1,0:T(8,128)(2,1)} %refs_0_.11, bf16[8,1024,512]{2,1,0:T(8,128)(2,1)} %collective-permute-done.8.refs_1_, bf16[8,1024,512]{2,1,0:T(8,128)(2,1)} %refs_2_.9, ...), custom_call_target="tpu_custom_call" | custom-call | flops 6442450944 | bytes 14680064 | tf_op jit(solution)/shard_map/gradients/pallas_call | solution.py:117
  112.0 3.3 %added.4.refs_4_ = bf16[3,512,256]{2,1,0:T(8,128)(2,1)} custom-call(s32[4]{0:T(128)} %pad_add_fusion.pos, f32[3,512,256]{2,1,0:T(8,128)} %get-tuple-element.67.refs_6_.keep_ref, bf16[3,128,256]{2,1,0:T(8,128)(2,1)} %collective-permute-done.24.refs_0_, bf16[3,128,256]{2,1,0:T(8,128)(2,1)} %collective-permute-done.25.refs_1_, ...), custom_call_target="tpu_custom_call" | custom-call | bytes 3000000 | tf_op jit(solution)/shard_map/added/pallas_call | solution.py:117
  121.1 11.8 %gradients.6 = (f32[3,512,256]{2,1,0:T(8,128)}, bf16[3,512,256]{2,1,0:T(8,128)(2,1)}) custom-call(s32[4]{0:T(128)} %pad_add_fusion.pos, bf16[8,1024,512]{2,1,0:T(8,128)(2,1)} %refs_0_.11, bf16[8,1024,512]{2,1,0:T(8,128)(2,1)} %collective-permute-done.8.refs_1_, bf16[8,1024,512]{2,1,0:T(8,128)(2,1)} %refs_2_.9, ...), custom_call_target="tpu_custom_call" | custom-call | flops 6442450944 | bytes 14680064 | tf_op jit(solution)/shard_map/gradients/pallas_call | solution.py:117
  135.9 3.6 %added.5.refs_8_ = bf16[3,512,256]{2,1,0:T(8,128)(2,1)} custom-call(s32[4]{0:T(128)} %pad_add_fusion.pos, f32[3,512,256]{2,1,0:T(8,128)} %get-tuple-element.77.refs_4_.keep_ref, bf16[3,512,256]{2,1,0:T(8,128)(2,1)} %collective-permute-done.30.refs_0_, bf16[3,512,256]{2,1,0:T(8,128)(2,1)} %collective-permute-done.31.refs_1_, ...), custom_call_target="tpu_custom_call" | custom-call | bytes 3000000 | tf_op jit(solution)/shard_map/added/pallas_call | solution.py:117
  139.5 12.5 %gradients.7 = (f32[3,512,256]{2,1,0:T(8,128)}, bf16[3,512,256]{2,1,0:T(8,128)(2,1)}, bf16[3,512,256]{2,1,0:T(8,128)(2,1)}, f32[8,512]{1,0:T(8,128)}) custom-call(s32[4]{0:T(128)} %pad_add_fusion.pos, bf16[8,1024,512]{2,1,0:T(8,128)(2,1)} %refs_0_.11, bf16[8,1024,512]{2,1,0:T(8,128)(2,1)} %collective-permute-done.8.refs_1_, bf16[8,1024,512]{2,1,0:T(8,128)(2,1)} %refs_2_.9, ...), custom_call_target="tpu_custom_call" | custom-call | flops 6442450944 | bytes 14680064 | tf_op jit(solution)/shard_map/gradients/pallas_call | solution.py:117
  157.6 17.9 %collective-permute-done.32.refs_0_ = bf16[3,512,256]{2,1,0:T(8,128)(2,1)} collective-permute-done((bf16[3,512,256]{2,1,0:T(8,128)(2,1)}, bf16[3,512,256]{2,1,0:T(8,128)(2,1)}, u32[]{:S(2)}, u32[]{:S(2)}) %collective-permute-start.32) | collective-permute-done | bytes 786464 | tf_op jit(solution)/shard_map/ppermute | solution.py:530
  175.5 3.6 %added.7.keep_ref = f32[3,512,256]{2,1,0:T(8,128)} custom-call(s32[4]{0:T(128)} %pad_add_fusion.pos, f32[3,512,256]{2,1,0:T(8,128)} %get-tuple-element.80.refs_1_.keep_ref, bf16[3,512,256]{2,1,0:T(8,128)(2,1)} %collective-permute-done.32.refs_0_, bf16[3,512,256]{2,1,0:T(8,128)(2,1)} %added.6.refs_1_), custom_call_target="tpu_custom_call" | custom-call | bytes 24000000 | tf_op jit(solution)/shard_map/added/pallas_call | solution.py:117
  179.1 11.1 %collective-permute-done.35.refs_1_ = bf16[3,512,256]{2,1,0:T(8,128)(2,1)} collective-permute-done((bf16[3,512,256]{2,1,0:T(8,128)(2,1)}, bf16[3,512,256]{2,1,0:T(8,128)(2,1)}, u32[]{:S(2)}, u32[]{:S(2)}) %collective-permute-start.35) | collective-permute-done | bytes 786464 | tf_op jit(solution)/shard_map/ppermute | solution.py:530
  190.3 4.2 %total_gradient.1 = (f32[3,512,256]{2,1,0:T(8,128)}, f32[8,128]{1,0:T(8,128)}) custom-call(s32[4]{0:T(128)} %pad_add_fusion.pos, f32[3,512,256]{2,1,0:T(8,128)} %added.7.keep_ref, bf16[3,512,256]{2,1,0:T(8,128)(2,1)} %collective-permute-done.34.refs_0_, bf16[3,512,256]{2,1,0:T(8,128)(2,1)} %collective-permute-done.35.refs_1_), custom_call_target="tpu_custom_call" | custom-call | tf_op jit(solution)/shard_map/total_gradient/pallas_call | solution.py:117
  198.4 3.8 %renewed_block.1.held_ref = bf16[3,512,256]{2,1,0:T(8,128)(2,1)} custom-call(s32[4]{0:T(128)} %pad_add_fusion.pos, f32[3,512,256]{2,1,0:T(8,128)} %get-tuple-element.83.g_ref, bf16[3,512,256]{2,1,0:T(8,128)(2,1)} %get-tuple-element.84.w_ref, f32[8,512]{1,0:T(8,128)} %get-tuple-element.85.sq_ref, f32[8,128]{1,0:T(8,128)} %get-tuple-element.86.sums_ref, ...), custom_call_target="tpu_custom_call" | custom-call | tf_op jit(solution)/shard_map/renewed_block/pallas_call | solution.py:117
  205.3 31.4 %collective-permute-done.39.refs_1_.held_ref = bf16[3,512,256]{2,1,0:T(8,128)(2,1)} collective-permute-done((bf16[3,512,256]{2,1,0:T(8,128)(2,1)}, bf16[3,512,256]{2,1,0:T(8,128)(2,1)}, u32[]{:S(2)}, u32[]{:S(2)}) %collective-permute-start.39) | collective-permute-done | bytes 786464 | tf_op jit(solution)/shard_map/ppermute | solution.py:530
  238.1 7.4 %apply_renewed.4 = (bf16[8,1024,512]{2,1,0:T(8,128)(2,1)}, bf16[1024,512]{1,0:T(8,128)(2,1)}) custom-call(s32[4]{0:T(128)} %pad_add_fusion.pos, bf16[8,1024,512]{2,1,0:T(8,128)(2,1)} %q0.7, bf16[4,1024,512]{2,1,0:T(8,128)(2,1)} %collective-permute-done.7.q1, bf16[3,512,256]{2,1,0:T(8,128)(2,1)} %renewed_block.1.held_ref, ...), custom_call_target="tpu_custom_call" | custom-call | flops 3221225472 | bytes 7340032 | tf_op jit(solution)/shard_map/apply_renewed/pallas_call | solution.py:117
  245.6 10.3 %collective-permute-done.40.rest_0_.refs_1_.held_ref = bf16[3,512,256]{2,1,0:T(8,128)(2,1)} collective-permute-done((bf16[3,512,256]{2,1,0:T(8,128)(2,1)}, bf16[3,512,256]{2,1,0:T(8,128)(2,1)}, u32[]{:S(2)}, u32[]{:S(2)}) %collective-permute-start.40) | collective-permute-done | bytes 786464 | tf_op jit(solution)/shard_map/ppermute | solution.py:530
  260.8 7.4 %apply_renewed.5 = (bf16[8,1024,512]{2,1,0:T(8,128)(2,1)}, bf16[1024,512]{1,0:T(8,128)(2,1)}) custom-call(s32[4]{0:T(128)} %pad_add_fusion.pos, bf16[8,1024,512]{2,1,0:T(8,128)(2,1)} %q0.7, bf16[4,1024,512]{2,1,0:T(8,128)(2,1)} %collective-permute-done.7.q1, ...), custom_call_target="tpu_custom_call", output_to_operand_aliasing={{0}: (6, {})} | custom-call | flops 3221225472 | bytes 7340032 | tf_op jit(solution)/shard_map/apply_renewed/pallas_call | solution.py:117
  268.3 8.5 %collective-permute-done.41.swapped_ref = bf16[3,512,256]{2,1,0:T(8,128)(2,1)} collective-permute-done((bf16[3,512,256]{2,1,0:T(8,128)(2,1)}, bf16[3,512,256]{2,1,0:T(8,128)(2,1)}, u32[]{:S(2)}, u32[]{:S(2)}) %collective-permute-start.41) | collective-permute-done | bytes 786464 | tf_op jit(solution)/shard_map/ppermute | solution.py:530
  278.0 7.4 %apply_renewed.6 = (bf16[8,1024,512]{2,1,0:T(8,128)(2,1)}, bf16[1024,512]{1,0:T(8,128)(2,1)}) custom-call(s32[4]{0:T(128)} %pad_add_fusion.pos, bf16[8,1024,512]{2,1,0:T(8,128)(2,1)} %q0.7, bf16[4,1024,512]{2,1,0:T(8,128)(2,1)} %collective-permute-done.7.q1, ...), custom_call_target="tpu_custom_call", output_to_operand_aliasing={{0}: (8, {})} | custom-call | flops 3221225472 | bytes 7340032 | tf_op jit(solution)/shard_map/apply_renewed/pallas_call | solution.py:117
  285.5 7.4 %apply_renewed.7 = (bf16[8,1024,512]{2,1,0:T(8,128)(2,1)}, bf16[1024,512]{1,0:T(8,128)(2,1)}) custom-call(s32[4]{0:T(128)} %pad_add_fusion.pos, bf16[8,1024,512]{2,1,0:T(8,128)(2,1)} %q0.7, bf16[4,1024,512]{2,1,0:T(8,128)(2,1)} %collective-permute-done.7.q1, ...), custom_call_target="tpu_custom_call", output_to_operand_aliasing={{0}: (6, {})} | custom-call | flops 3221225472 | bytes 7340032 | tf_op jit(solution)/shard_map/apply_renewed/pallas_call | solution.py:117
  (102 shorter events, 92.7 us)
Async XLA Ops:
  0.0 65.2 %collective-permute-start.8 = (bf16[8,1024,512]{2,1,0:T(8,128)(2,1)}, bf16[8,1024,512]{2,1,0:T(8,128)(2,1)}, u32[]{:S(2)}, u32[]{:S(2)}) collective-permute-start(bf16[8,1024,512]{2,1,0:T(8,128)(2,1)} %refs_0_.11), channel_id=1, source_target_pairs={{0,1},{1,0},{2,3},{3,2},{4,5},{5,4},{6,7},{7,6},{8,9},{9,8},{10,11... | collective-permute-start | bytes 25165832 | tf_op jit(solution)/shard_map/ppermute | solution.py:521
  0.5 68.0 %collective-permute-start.9 = (bf16[8,1024,512]{2,1,0:T(8,128)(2,1)}, bf16[8,1024,512]{2,1,0:T(8,128)(2,1)}, u32[]{:S(2)}, u32[]{:S(2)}) collective-permute-start(bf16[8,1024,512]{2,1,0:T(8,128)(2,1)} %refs_2_.9), channel_id=1, source_target_pairs={{0,1},{1,0},{2,3},{3,2},{4,5},{5,4},{6,7},{7,6},{8,9},{9,8},{10,11... | collective-permute-start | bytes 25165832 | tf_op jit(solution)/shard_map/ppermute | solution.py:521
  62.5 22.0 %collective-permute-start.20 = (bf16[4,3,128,256]{3,2,1,0:T(8,128)(2,1)}, bf16[4,3,128,256]{3,2,1,0:T(8,128)(2,1)}, u32[]{:S(2)}, u32[]{:S(2)}) collective-permute-start(bf16[4,3,128,256]{3,2,1,0:T(8,128)(2,1)} %get-tuple-element.66.refs_10_.refs_6_), channel_id=1, source_target_pairs={{0,16},{16,0},{1,17},{17,1},{2,18},{18,2},{3,19},{19,3},{4,20},{20... | collective-permute-start | bytes 2359304 | tf_op jit(solution)/shard_map/ppermute | solution.py:524
  65.2 18.8 %collective-permute-start.19 = (bf16[3,128,256]{2,1,0:T(8,128)(2,1)}, bf16[3,128,256]{2,1,0:T(8,128)(2,1)}, u32[]{:S(2)}, u32[]{:S(2)}) collective-permute-start(bf16[3,128,256]{2,1,0:T(8,128)(2,1)} %get-tuple-element.65), channel_id=1, source_target_pairs={{0,12},{2,14},{4,8},{6,10},{8,4},{10,6},{12,0},{14,2},{1,13},{3,15... | collective-permute-start | bytes 589832 | tf_op jit(solution)/shard_map/ppermute | solution.py:530
  87.9 28.9 %collective-permute-start.28 = (bf16[4,3,128,256]{3,2,1,0:T(8,128)(2,1)}, bf16[4,3,128,256]{3,2,1,0:T(8,128)(2,1)}, u32[]{:S(2)}, u32[]{:S(2)}) collective-permute-start(bf16[4,3,128,256]{3,2,1,0:T(8,128)(2,1)} %get-tuple-element.76.refs_8_.refs_6_), channel_id=1, source_target_pairs={{0,16},{16,0},{1,17},{17,1},{2,18},{18,2},{3,19},{19,3},{4,20},{20... | collective-permute-start | bytes 2359304 | tf_op jit(solution)/shard_map/ppermute | solution.py:524
  95.7 142.4 %collective-permute-start.7 = (bf16[4,1024,512]{2,1,0:T(8,128)(2,1)}, bf16[4,1024,512]{2,1,0:T(8,128)(2,1)}, u32[]{:S(2)}, u32[]{:S(2)}) collective-permute-start(bf16[4,1024,512]{2,1,0:T(8,128)(2,1)} %other_half.1), channel_id=1, source_target_pairs={{0,1},{1,0},{2,3},{3,2},{4,5},{5,4},{6,7},{7,6},{8,9},{9,8},{10,11... | collective-permute-start | bytes 12582920 | tf_op jit(solution)/shard_map/ppermute | solution.py:521
  95.7 19.6 %collective-permute-start.21 = (bf16[3,128,256]{2,1,0:T(8,128)(2,1)}, bf16[3,128,256]{2,1,0:T(8,128)(2,1)}, u32[]{:S(2)}, u32[]{:S(2)}) collective-permute-start(bf16[3,128,256]{2,1,0:T(8,128)(2,1)} %get-tuple-element.69), channel_id=1, source_target_pairs={{0,4},{2,6},{4,0},{6,2},{8,12},{10,14},{12,8},{14,10},{1,5},{3,7},... | collective-permute-start | bytes 589832 | tf_op jit(solution)/shard_map/ppermute | solution.py:530
  96.3 20.4 %collective-permute-start.22 = (bf16[3,128,256]{2,1,0:T(8,128)(2,1)}, bf16[3,128,256]{2,1,0:T(8,128)(2,1)}, u32[]{:S(2)}, u32[]{:S(2)}) collective-permute-start(bf16[3,128,256]{2,1,0:T(8,128)(2,1)} %get-tuple-element.70), channel_id=1, source_target_pairs={{0,8},{2,10},{4,12},{6,14},{8,0},{10,2},{12,4},{14,6},{1,9},{3,11}... | collective-permute-start | bytes 589832 | tf_op jit(solution)/shard_map/ppermute | solution.py:530
  97.6 19.2 %collective-permute-start.23 = (bf16[3,128,256]{2,1,0:T(8,128)(2,1)}, bf16[3,128,256]{2,1,0:T(8,128)(2,1)}, u32[]{:S(2)}, u32[]{:S(2)}) collective-permute-start(bf16[3,128,256]{2,1,0:T(8,128)(2,1)} %get-tuple-element.71), channel_id=1, source_target_pairs={{0,12},{2,14},{4,8},{6,10},{8,4},{10,6},{12,0},{14,2},{1,13},{3,15... | collective-permute-start | bytes 589832 | tf_op jit(solution)/shard_map/ppermute | solution.py:530
  115.3 19.4 %collective-permute-start.30 = (bf16[3,512,256]{2,1,0:T(8,128)(2,1)}, bf16[3,512,256]{2,1,0:T(8,128)(2,1)}, u32[]{:S(2)}, u32[]{:S(2)}) collective-permute-start(bf16[3,512,256]{2,1,0:T(8,128)(2,1)} %get-tuple-element.78), channel_id=1, source_target_pairs={{0,2},{2,0},{4,6},{6,4},{8,10},{10,8},{12,14},{14,12},{1,3},{3,1},... | collective-permute-start | bytes 2359304 | tf_op jit(solution)/shard_map/ppermute | solution.py:527
  116.8 19.1 %collective-permute-start.31 = (bf16[3,512,256]{2,1,0:T(8,128)(2,1)}, bf16[3,512,256]{2,1,0:T(8,128)(2,1)}, u32[]{:S(2)}, u32[]{:S(2)}) collective-permute-start(bf16[3,512,256]{2,1,0:T(8,128)(2,1)} %added.4.refs_4_), channel_id=1, source_target_pairs={{0,4},{2,6},{4,0},{6,2},{8,12},{10,14},{12,8},{14,10},{1,5},{3,7},... | collective-permute-start | bytes 2359304 | tf_op jit(solution)/shard_map/ppermute | solution.py:530
  119.6 19.9 %collective-permute-start.29 = (bf16[4,3,128,256]{3,2,1,0:T(8,128)(2,1)}, bf16[4,3,128,256]{3,2,1,0:T(8,128)(2,1)}, u32[]{:S(2)}, u32[]{:S(2)}) collective-permute-start(bf16[4,3,128,256]{3,2,1,0:T(8,128)(2,1)} %next_pieces.7.refs_8_.refs_6_), channel_id=1, source_target_pairs={{0,16},{16,0},{1,17},{17,1},{2,18},{18,2},{3,19},{19,3},{4,20},{20... | collective-permute-start | bytes 2359304 | tf_op jit(solution)/shard_map/ppermute | solution.py:524
  132.9 19.1 %collective-permute-start.33 = (bf16[3,512,256]{2,1,0:T(8,128)(2,1)}, bf16[3,512,256]{2,1,0:T(8,128)(2,1)}, u32[]{:S(2)}, u32[]{:S(2)}) collective-permute-start(bf16[3,512,256]{2,1,0:T(8,128)(2,1)} %get-tuple-element.81), channel_id=1, source_target_pairs={{0,2},{2,0},{4,6},{6,4},{8,10},{10,8},{12,14},{14,12},{1,3},{3,1},... | collective-permute-start | bytes 2359304 | tf_op jit(solution)/shard_map/ppermute | solution.py:527
  139.5 36.0 %collective-permute-start.32 = (bf16[3,512,256]{2,1,0:T(8,128)(2,1)}, bf16[3,512,256]{2,1,0:T(8,128)(2,1)}, u32[]{:S(2)}, u32[]{:S(2)}) collective-permute-start(bf16[3,512,256]{2,1,0:T(8,128)(2,1)} %added.5.refs_8_), channel_id=1, source_target_pairs={{0,8},{2,10},{4,12},{6,14},{8,0},{10,2},{12,4},{14,6},{1,9},{3,11}... | collective-permute-start | bytes 2359304 | tf_op jit(solution)/shard_map/ppermute | solution.py:530
  155.4 34.9 %collective-permute-start.35 = (bf16[3,512,256]{2,1,0:T(8,128)(2,1)}, bf16[3,512,256]{2,1,0:T(8,128)(2,1)}, u32[]{:S(2)}, u32[]{:S(2)}) collective-permute-start(bf16[3,512,256]{2,1,0:T(8,128)(2,1)} %added.6.refs_1_), channel_id=1, source_target_pairs={{0,4},{2,6},{4,0},{6,2},{8,12},{10,14},{12,8},{14,10},{1,5},{3,7},... | collective-permute-start | bytes 2359304 | tf_op jit(solution)/shard_map/ppermute | solution.py:530
  156.8 33.4 %collective-permute-start.34 = (bf16[3,512,256]{2,1,0:T(8,128)(2,1)}, bf16[3,512,256]{2,1,0:T(8,128)(2,1)}, u32[]{:S(2)}, u32[]{:S(2)}) collective-permute-start(bf16[3,512,256]{2,1,0:T(8,128)(2,1)} %get-tuple-element.82), channel_id=1, source_target_pairs={{0,2},{2,0},{4,6},{6,4},{8,10},{10,8},{12,14},{14,12},{1,3},{3,1},... | collective-permute-start | bytes 2359304 | tf_op jit(solution)/shard_map/ppermute | solution.py:527
  202.1 34.6 %collective-permute-start.39 = (bf16[3,512,256]{2,1,0:T(8,128)(2,1)}, bf16[3,512,256]{2,1,0:T(8,128)(2,1)}, u32[]{:S(2)}, u32[]{:S(2)}) collective-permute-start(bf16[3,512,256]{2,1,0:T(8,128)(2,1)} %renewed_block.1.held_ref), channel_id=1, source_target_pairs={{0,8},{2,10},{4,12},{6,14},{8,0},{10,2},{12,4},{14,6},{1,9},{3,11}... | collective-permute-start | bytes 2359304 | tf_op jit(solution)/shard_map/ppermute | solution.py:530
  202.1 36.0 %collective-permute-start.37 = (bf16[3,512,256]{2,1,0:T(8,128)(2,1)}, bf16[3,512,256]{2,1,0:T(8,128)(2,1)}, u32[]{:S(2)}, u32[]{:S(2)}) collective-permute-start(bf16[3,512,256]{2,1,0:T(8,128)(2,1)} %renewed_block.1.held_ref), channel_id=1, source_target_pairs={{0,4},{2,6},{4,0},{6,2},{8,12},{10,14},{12,8},{14,10},{1,5},{3,7},... | collective-permute-start | bytes 2359304 | tf_op jit(solution)/shard_map/ppermute | solution.py:530
  204.5 33.6 %collective-permute-start.38 = (bf16[3,512,256]{2,1,0:T(8,128)(2,1)}, bf16[3,512,256]{2,1,0:T(8,128)(2,1)}, u32[]{:S(2)}, u32[]{:S(2)}) collective-permute-start(bf16[3,512,256]{2,1,0:T(8,128)(2,1)} %renewed_block.1.held_ref), channel_id=1, source_target_pairs={{0,2},{2,0},{4,6},{6,4},{8,10},{10,8},{12,14},{14,12},{1,3},{3,1},... | collective-permute-start | bytes 2359304 | tf_op jit(solution)/shard_map/ppermute | solution.py:527
  236.7 19.1 %collective-permute-start.40 = (bf16[3,512,256]{2,1,0:T(8,128)(2,1)}, bf16[3,512,256]{2,1,0:T(8,128)(2,1)}, u32[]{:S(2)}, u32[]{:S(2)}) collective-permute-start(bf16[3,512,256]{2,1,0:T(8,128)(2,1)} %collective-permute-done.39.refs_1_.held_ref), channel_id=1, source_target_pairs={{0,4},{2,6},{4,0},{6,2},{8,12},{10,14},{12,8},{14,10},{1,5},{3,7},... | collective-permute-start | bytes 2359304 | tf_op jit(solution)/shard_map/ppermute | solution.py:530
  236.7 24.1 %collective-permute-start.44 = (bf16[3,512,256]{2,1,0:T(8,128)(2,1)}, bf16[3,512,256]{2,1,0:T(8,128)(2,1)}, u32[]{:S(2)}, u32[]{:S(2)}) collective-permute-start(bf16[3,512,256]{2,1,0:T(8,128)(2,1)} %collective-permute-done.39.refs_1_.held_ref), channel_id=1, source_target_pairs={{0,2},{2,0},{4,6},{6,4},{8,10},{10,8},{12,14},{14,12},{1,3},{3,1},... | collective-permute-start | bytes 2359304 | tf_op jit(solution)/shard_map/ppermute | solution.py:527
  245.5 22.8 %collective-permute-start.42 = (bf16[1024,512]{1,0:T(8,128)(2,1)}, bf16[1024,512]{1,0:T(8,128)(2,1)}, u32[]{:S(2)}, u32[]{:S(2)}) collective-permute-start(bf16[1024,512]{1,0:T(8,128)(2,1)} %get-tuple-element.88), channel_id=1, source_target_pairs={{0,1},{1,0},{2,3},{3,2},{4,5},{5,4},{6,7},{7,6},{8,9},{9,8},{10,11... | collective-permute-start | bytes 3145736 | tf_op jit(solution)/shard_map/ppermute | solution.py:521
  258.6 18.2 %collective-permute-start.41 = (bf16[3,512,256]{2,1,0:T(8,128)(2,1)}, bf16[3,512,256]{2,1,0:T(8,128)(2,1)}, u32[]{:S(2)}, u32[]{:S(2)}) collective-permute-start(bf16[3,512,256]{2,1,0:T(8,128)(2,1)} %copied.1.refs_0_), channel_id=1, source_target_pairs={{0,4},{2,6},{4,0},{6,2},{8,12},{10,14},{12,8},{14,10},{1,5},{3,7},... | collective-permute-start | bytes 2359304 | tf_op jit(solution)/shard_map/ppermute | solution.py:530
  258.9 19.1 %collective-permute-start.43 = (bf16[3,512,256]{2,1,0:T(8,128)(2,1)}, bf16[3,512,256]{2,1,0:T(8,128)(2,1)}, u32[]{:S(2)}, u32[]{:S(2)}) collective-permute-start(bf16[3,512,256]{2,1,0:T(8,128)(2,1)} %collective-permute-done.40.rest_0_.refs_1_.held_ref), channel_id=1, source_target_pairs={{0,2},{2,0},{4,6},{6,4},{8,10},{10,8},{12,14},{14,12},{1,3},{3,1},... | collective-permute-start | bytes 2359304 | tf_op jit(solution)/shard_map/ppermute | solution.py:527
  (27 other events, 266.1 us)
where the time goes:
time: 300 us; the launch traced here: 299 us
  Pallas kernels  131 us (44%)
  waiting for transfers between devices  114 us (38%)
  starting transfers between devices  52.2 us (17%)
    pallas_call x23, Pallas kernels, call(): pl.pallas_call(body, name=name, out_shape=out_shapes, grid_spec=pltpu.Pre...  131 us
    ppermute x19, waiting for transfers between devices, over_z(): return lax.ppermute(a, 'seq', [(i, i ^ 2 * j) for i in range(8)])  93.8 us
    ppermute x19, starting transfers between devices, over_z(): return lax.ppermute(a, 'seq', [(i, i ^ 2 * j) for i in range(8)])  27.7 us
    ppermute x13, starting transfers between devices, over_x(): return lax.ppermute(a, 'seq', [(i, i ^ 1) for i in range(8)])  15.7 us
    ppermute x11, waiting for transfers between devices, over_sub(): return lax.ppermute(a, 'sub', flip)  13.2 us
    ppermute x5, starting transfers between devices, over_groups(): return lax.ppermute(a, 'groups', flip)  6.58 us
  transfers between devices with their start and end apart: 48, of which 23 were waited for; matrix products, arithmetic and copies ran while one was open for 0% of the time, Pallas kernels for 43%

commit v1 on v0

--- a/solution.py
+++ b/solution.py
@@ -193,12 +193,15 @@
     )
 
 
-def copied(positions, array, after):
-    def body(pos, in_ref, *rest):
-        rest[-1][...] = in_ref[...]
-
-    shape = sds(array.shape, BF16)
-    return call(body, "copied", positions, (1,), (array, *after), [whole(array)] + [anywhere()] * len(after), shape, whole(shape))
+def handed_on(positions, array, after):
+    def body(pos, *refs):
+        refs[-1][...] = jnp.zeros_like(refs[-1])
+
+    shapes = [sds(array.shape, BF16), sds((8, 128), F32)]
+    return call(
+        body, "handed_on", positions, (1,), (array, *after), [anywhere()] * (1 + len(after)), shapes,
+        [anywhere(), whole(shapes[1])], aliases={1: 0},
+    )
 
 
 def token_rates(positions, codes, half, after):
@@ -430,31 +433,24 @@
         for copy in weights:
             copy.wait()
 
-        @pl.loop(0, chunks)
-        def _(c):
-            here = pl.ds(pl.multiple_of(c * tile, tile), tile)
-            there = pl.ds(pl.multiple_of(lax.rem(c * tile, tokens), tile), tile)
-            pltpu.make_async_copy(q1.at[heads_of[1], pl.ds(0, tile)], query.at[here], sems_q.at[c]).wait()
-            q = query[here, :]
-            gate = jnp.dot(q, w[0], preferred_element_type=F32)
-            up = jnp.dot(q, w[1], preferred_element_type=F32)
+        for n in range(len(blocks)):
+            late_in[n].wait()
+            late_out[n].start()
+        for copy in loads:
+            copy.wait()
+
+        def front(c):
+            q = query[c * tile : (c + 1) * tile, :]
+            return jnp.dot(q, w[0], preferred_element_type=F32), jnp.dot(q, w[1], preferred_element_type=F32)
+
+        following = front(0)
+        for c in range(chunks):
+            gate, up = following
+            if c + 1 < chunks:
+                following = front(c + 1)
             hidden = (gate * (0.5 * jnp.tanh(0.5 * gate) + 0.5) * up).astype(BF16)
-            result[here, :] = jnp.dot(hidden, w[2], preferred_element_type=F32).astype(BF16)
-
-            @pl.when(c < chunks // 2)
-            def _():
-                pltpu.make_async_copy(result.at[here], out_ref.at[heads_of[0], there], sems_out.at[c]).start()
-
-            @pl.when(c >= chunks // 2)
-            def _():
-                pltpu.make_async_copy(result.at[here], send_ref.at[there], sems_out.at[c]).start()
-
-            @pl.when(c == 0)
-            def _():
-                for n in range(len(blocks)):
-                    late_in[n].wait()
-                    late_out[n].start()
-
+            result[c * tile : (c + 1) * tile, :] = jnp.dot(hidden, w[2], preferred_element_type=F32).astype(BF16)
+            stores[c].start()
         for copy in stores + late_out:
             copy.wait()
 
@@ -582,12 +578,13 @@
         return out, (k, over_sub(sent))
 
     out, late0 = head_output(0, None, (), (from1, from2))
-    swapped_late = copied(positions, swapped, (from3, out))
+    swapped_late, _ = handed_on(positions, swapped, (from3, out))
     matrices[1] = (from1, over_z(swapped_late, 1))
     out, late2 = head_output(2, out, (), (swapped_late,))
     out, late1 = head_output(1, out, (late0,), matrices[3])
     out, late3 = head_output(3, out, (late2,), ())
-    return place(positions, out, (late1, late3), half)
+    out = place(positions, out, (late1,), half)
+    return place(positions, out, (late3,), half)
 
 
 def solution(mesh):

time: 300 us -> 298 us (level)
    pallas_call x23 -> x24, Pallas kernels: 131 us -> 131 us  [call(): pl.pallas_call(body, name=name, out_shape=out_shapes, grid_spec=pltpu.Pre...]
  transfers between devices with their start and end apart: 48 -> 48, of which waited for: 23 -> 22; matrix products, arithmetic and copies ran while one was open for 0% -> 0% of each run, Pallas kernels for 43% -> 43%
where the time goes in v1:
time: 298 us; the launch traced here: 297 us
  Pallas kernels  131 us (44%)
  waiting for transfers between devices  112 us (38%)
  starting transfers between devices  52.1 us (17%)
    pallas_call x24, Pallas kernels, call(): pl.pallas_call(body, name=name, out_shape=out_shapes, grid_spec=pltpu.Pre...  131 us
    ppermute x19, waiting for transfers between devices, over_z(): return lax.ppermute(a, 'seq', [(i, i ^ 2 * j) for i in range(8)])  94.6 us
    ppermute x19, starting transfers between devices, over_z(): return lax.ppermute(a, 'seq', [(i, i ^ 2 * j) for i in range(8)])  27.2 us
    ppermute x13, starting transfers between devices, over_x(): return lax.ppermute(a, 'seq', [(i, i ^ 1) for i in range(8)])  16.1 us
    ppermute x11, waiting for transfers between devices, over_sub(): return lax.ppermute(a, 'sub', flip)  10.5 us
    ppermute x5, starting transfers between devices, over_groups(): return lax.ppermute(a, 'groups', flip)  6.59 us
  transfers between devices with their start and end apart: 48, of which 22 were waited for; matrix products, arithmetic and copies ran while one was open for 0% of the time, Pallas kernels for 43%

profile of v1, /device:TPU:0, one launch (start us, length us, event | category | flops | bytes accessed | tf_op | source)
XLA Modules:
  0.0 297.3 jit_solution(15657526093038960516)
XLA Ops:
  2.1 6.0 %collective-permute-done.refs_3_ = f32[8,32,512]{2,1,0:T(8,128)S(1)} collective-permute-done((f32[8,32,512]{2,1,0:T(8,128)}, f32[8,32,512]{2,1,0:T(8,128)S(1)}, u32[]{:S(2)}, u32[]{:S(2)}) %collective-permute-start) | collective-permute-done | bytes 524320 | tf_op jit(solution)/shard_map/ppermute | solution.py:517
  22.5 4.7 %collective-permute-start.5 = (bf16[3,64,256]{2,1,0:T(8,128)(2,1)}, bf16[3,64,256]{2,1,0:T(8,128)(2,1)}, u32[]{:S(2)}, u32[]{:S(2)}) collective-permute-start(bf16[3,64,256]{2,1,0:T(8,128)(2,1)} %get-tuple-element.54), channel_id=1, source_target_pairs={{0,12},{2,14},{4,8},{6,10},{8,4},{10,6},{12,0},{14,2},{1,13},{3,15... | collective-permute-start | bytes 294920 | tf_op jit(solution)/shard_map/ppermute | solution.py:526
  43.3 5.9 %collective-permute-done.12.refs_2_ = bf16[3,128,256]{2,1,0:T(8,128)(2,1)} collective-permute-done((bf16[3,128,256]{2,1,0:T(8,128)(2,1)}, bf16[3,128,256]{2,1,0:T(8,128)(2,1)}, u32[]{:S(2)}, u32[]{:S(2)}) %collective-permute-start.12) | collective-permute-done | bytes 196640 | tf_op jit(solution)/shard_map/ppermute | solution.py:526
  51.4 3.6 %token_rates.1 = (bf16[4,1024,128]{2,1,0:T(8,128)(2,1)}, bf16[4,1024,128]{2,1,0:T(8,128)(2,1)}) custom-call(s32[4]{0:T(128)} %pad_add_fusion.pos, s32[8,1024]{1,0:T(8,128)} %refs_0_.7, s32[8,1024]{1,0:T(8,128)} %collective-permute-done.10.refs_1_, bf16[4,3,64,256]{3,2,1,0:T(8,128)(2,1)} %get-tuple-element.56.rest_0_.refs_2_.refs_6_), custom_call_target="tpu_custom_call" | custom-call | tf_op jit(solution)/shard_map/token_rates/pallas_call | solution.py:117
  68.4 11.9 %gradients.4 = (f32[3,512,256]{2,1,0:T(8,128)}, bf16[3,128,256]{2,1,0:T(8,128)(2,1)}, bf16[3,128,256]{2,1,0:T(8,128)(2,1)}, bf16[3,128,256]{2,1,0:T(8,128)(2,1)}, bf16[3,128,256]{2,1,0:T(8,128)(2,1)}) custom-call(s32[4]{0:T(128)} %pad_add_fusion.pos, bf16[8,1024,512]{2,1,0:T(8,128)(2,1)} %refs_0_.11, bf16[8,1024,512]{2,1,0:T(8,128)(2,1)} %collective-permute-done.8.refs_1_, ...), custom_call_target="tpu_custom_call" | custom-call | flops 6442450944 | bytes 14680064 | tf_op jit(solution)/shard_map/gradients/pallas_call | solution.py:117
  84.5 3.3 %next_pieces.6 = (bf16[4,3,128,256]{3,2,1,0:T(8,128)(2,1)}, bf16[3,128,256]{2,1,0:T(8,128)(2,1)}, bf16[3,128,256]{2,1,0:T(8,128)(2,1)}, bf16[3,128,256]{2,1,0:T(8,128)(2,1)}, bf16[3,128,256]{2,1,0:T(8,128)(2,1)}) custom-call(s32[4]{0:T(128)} %pad_add_fusion.pos, bf16[3,128,256]{2,1,0:T(8,128)(2,1)} %get-tuple-element.63.refs_0_, ...), custom_call_target="tpu_custom_call" | custom-call | bytes 9000000 | tf_op jit(solution)/shard_map/next_pieces/pallas_call | solution.py:117
  88.3 7.3 %other_half.1 = bf16[4,1024,512]{2,1,0:T(8,128)(2,1)} custom-call(s32[4]{0:T(128)} %pad_add_fusion.pos, bf16[8,1024,512]{2,1,0:T(8,128)(2,1)} %q0.7, bf16[4,3,64,256]{3,2,1,0:T(8,128)(2,1)} %get-tuple-element.56.rest_0_.refs_2_.refs_6_), custom_call_target="tpu_custom_call" | custom-call | bytes 9000000 | tf_op jit(solution)/shard_map/other_half/pallas_call | solution.py:117
  100.1 11.8 %gradients.5 = (f32[3,512,256]{2,1,0:T(8,128)}, bf16[3,512,256]{2,1,0:T(8,128)(2,1)}) custom-call(s32[4]{0:T(128)} %pad_add_fusion.pos, bf16[8,1024,512]{2,1,0:T(8,128)(2,1)} %refs_0_.11, bf16[8,1024,512]{2,1,0:T(8,128)(2,1)} %collective-permute-done.8.refs_1_, bf16[8,1024,512]{2,1,0:T(8,128)(2,1)} %refs_2_.9, ...), custom_call_target="tpu_custom_call" | custom-call | flops 6442450944 | bytes 14680064 | tf_op jit(solution)/shard_map/gradients/pallas_call | solution.py:117
  111.9 3.3 %added.4.refs_4_ = bf16[3,512,256]{2,1,0:T(8,128)(2,1)} custom-call(s32[4]{0:T(128)} %pad_add_fusion.pos, f32[3,512,256]{2,1,0:T(8,128)} %get-tuple-element.68.refs_6_.keep_ref, bf16[3,128,256]{2,1,0:T(8,128)(2,1)} %collective-permute-done.24.refs_0_, bf16[3,128,256]{2,1,0:T(8,128)(2,1)} %collective-permute-done.25.refs_1_, ...), custom_call_target="tpu_custom_call" | custom-call | bytes 3000000 | tf_op jit(solution)/shard_map/added/pallas_call | solution.py:117
  121.0 11.8 %gradients.6 = (f32[3,512,256]{2,1,0:T(8,128)}, bf16[3,512,256]{2,1,0:T(8,128)(2,1)}) custom-call(s32[4]{0:T(128)} %pad_add_fusion.pos, bf16[8,1024,512]{2,1,0:T(8,128)(2,1)} %refs_0_.11, bf16[8,1024,512]{2,1,0:T(8,128)(2,1)} %collective-permute-done.8.refs_1_, bf16[8,1024,512]{2,1,0:T(8,128)(2,1)} %refs_2_.9, ...), custom_call_target="tpu_custom_call" | custom-call | flops 6442450944 | bytes 14680064 | tf_op jit(solution)/shard_map/gradients/pallas_call | solution.py:117
  135.8 3.6 %added.5.refs_8_ = bf16[3,512,256]{2,1,0:T(8,128)(2,1)} custom-call(s32[4]{0:T(128)} %pad_add_fusion.pos, f32[3,512,256]{2,1,0:T(8,128)} %get-tuple-element.78.refs_4_.keep_ref, bf16[3,512,256]{2,1,0:T(8,128)(2,1)} %collective-permute-done.30.refs_0_, bf16[3,512,256]{2,1,0:T(8,128)(2,1)} %collective-permute-done.31.refs_1_, ...), custom_call_target="tpu_custom_call" | custom-call | bytes 3000000 | tf_op jit(solution)/shard_map/added/pallas_call | solution.py:117
  139.4 12.5 %gradients.7 = (f32[3,512,256]{2,1,0:T(8,128)}, bf16[3,512,256]{2,1,0:T(8,128)(2,1)}, bf16[3,512,256]{2,1,0:T(8,128)(2,1)}, f32[8,512]{1,0:T(8,128)}) custom-call(s32[4]{0:T(128)} %pad_add_fusion.pos, bf16[8,1024,512]{2,1,0:T(8,128)(2,1)} %refs_0_.11, bf16[8,1024,512]{2,1,0:T(8,128)(2,1)} %collective-permute-done.8.refs_1_, bf16[8,1024,512]{2,1,0:T(8,128)(2,1)} %refs_2_.9, ...), custom_call_target="tpu_custom_call" | custom-call | flops 6442450944 | bytes 14680064 | tf_op jit(solution)/shard_map/gradients/pallas_call | solution.py:117
  157.5 17.9 %collective-permute-done.32.refs_0_ = bf16[3,512,256]{2,1,0:T(8,128)(2,1)} collective-permute-done((bf16[3,512,256]{2,1,0:T(8,128)(2,1)}, bf16[3,512,256]{2,1,0:T(8,128)(2,1)}, u32[]{:S(2)}, u32[]{:S(2)}) %collective-permute-start.32) | collective-permute-done | bytes 786464 | tf_op jit(solution)/shard_map/ppermute | solution.py:526
  175.4 3.6 %added.7.keep_ref = f32[3,512,256]{2,1,0:T(8,128)} custom-call(s32[4]{0:T(128)} %pad_add_fusion.pos, f32[3,512,256]{2,1,0:T(8,128)} %get-tuple-element.81.refs_1_.keep_ref, bf16[3,512,256]{2,1,0:T(8,128)(2,1)} %collective-permute-done.32.refs_0_, bf16[3,512,256]{2,1,0:T(8,128)(2,1)} %added.6.refs_1_), custom_call_target="tpu_custom_call" | custom-call | bytes 24000000 | tf_op jit(solution)/shard_map/added/pallas_call | solution.py:117
  179.0 11.1 %collective-permute-done.35.refs_1_ = bf16[3,512,256]{2,1,0:T(8,128)(2,1)} collective-permute-done((bf16[3,512,256]{2,1,0:T(8,128)(2,1)}, bf16[3,512,256]{2,1,0:T(8,128)(2,1)}, u32[]{:S(2)}, u32[]{:S(2)}) %collective-permute-start.35) | collective-permute-done | bytes 786464 | tf_op jit(solution)/shard_map/ppermute | solution.py:526
  190.2 4.2 %total_gradient.1 = (f32[3,512,256]{2,1,0:T(8,128)}, f32[8,128]{1,0:T(8,128)}) custom-call(s32[4]{0:T(128)} %pad_add_fusion.pos, f32[3,512,256]{2,1,0:T(8,128)} %added.7.keep_ref, bf16[3,512,256]{2,1,0:T(8,128)(2,1)} %collective-permute-done.34.refs_0_, bf16[3,512,256]{2,1,0:T(8,128)(2,1)} %collective-permute-done.35.refs_1_), custom_call_target="tpu_custom_call" | custom-call | tf_op jit(solution)/shard_map/total_gradient/pallas_call | solution.py:117
  198.2 3.8 %renewed_block.1.held_ref = bf16[3,512,256]{2,1,0:T(8,128)(2,1)} custom-call(s32[4]{0:T(128)} %pad_add_fusion.pos, f32[3,512,256]{2,1,0:T(8,128)} %get-tuple-element.84.g_ref, bf16[3,512,256]{2,1,0:T(8,128)(2,1)} %get-tuple-element.85.w_ref, f32[8,512]{1,0:T(8,128)} %get-tuple-element.86.sq_ref, f32[8,128]{1,0:T(8,128)} %get-tuple-element.87.sums_ref, ...), custom_call_target="tpu_custom_call" | custom-call | tf_op jit(solution)/shard_map/renewed_block/pallas_call | solution.py:117
  205.2 31.4 %collective-permute-done.37.refs_1_.held_ref = bf16[3,512,256]{2,1,0:T(8,128)(2,1)} collective-permute-done((bf16[3,512,256]{2,1,0:T(8,128)(2,1)}, bf16[3,512,256]{2,1,0:T(8,128)(2,1)}, u32[]{:S(2)}, u32[]{:S(2)}) %collective-permute-start.37) | collective-permute-done | bytes 786464 | tf_op jit(solution)/shard_map/ppermute | solution.py:526
  238.0 7.0 %apply_renewed.4 = (bf16[8,1024,512]{2,1,0:T(8,128)(2,1)}, bf16[1024,512]{1,0:T(8,128)(2,1)}) custom-call(s32[4]{0:T(128)} %pad_add_fusion.pos, bf16[8,1024,512]{2,1,0:T(8,128)(2,1)} %q0.7, bf16[4,1024,512]{2,1,0:T(8,128)(2,1)} %collective-permute-done.7.q1, bf16[3,512,256]{2,1,0:T(8,128)(2,1)} %renewed_block.1.held_ref, ...), custom_call_target="tpu_custom_call" | custom-call | flops 3221225472 | bytes 7340032 | tf_op jit(solution)/shard_map/apply_renewed/pallas_call | solution.py:117
  245.1 10.6 %collective-permute-done.38.refs_1_.held_ref = bf16[3,512,256]{2,1,0:T(8,128)(2,1)} collective-permute-done((bf16[3,512,256]{2,1,0:T(8,128)(2,1)}, bf16[3,512,256]{2,1,0:T(8,128)(2,1)}, u32[]{:S(2)}, u32[]{:S(2)}) %collective-permute-start.38) | collective-permute-done | bytes 786464 | tf_op jit(solution)/shard_map/ppermute | solution.py:526
  259.2 7.0 %apply_renewed.5 = (bf16[8,1024,512]{2,1,0:T(8,128)(2,1)}, bf16[1024,512]{1,0:T(8,128)(2,1)}) custom-call(s32[4]{0:T(128)} %pad_add_fusion.pos, bf16[8,1024,512]{2,1,0:T(8,128)(2,1)} %q0.7, bf16[4,1024,512]{2,1,0:T(8,128)(2,1)} %collective-permute-done.7.q1, ...), custom_call_target="tpu_custom_call", output_to_operand_aliasing={{0}: (6, {})} | custom-call | flops 3221225472 | bytes 7340032 | tf_op jit(solution)/shard_map/apply_renewed/pallas_call | solution.py:117
  266.4 8.9 %collective-permute-done.44.swapped_ref = bf16[3,512,256]{2,1,0:T(8,128)(2,1)} collective-permute-done((bf16[3,512,256]{2,1,0:T(8,128)(2,1)}, bf16[3,512,256]{2,1,0:T(8,128)(2,1)}, u32[]{:S(2)}, u32[]{:S(2)}) %collective-permute-start.44) | collective-permute-done | bytes 786464 | tf_op jit(solution)/shard_map/ppermute | solution.py:526
  276.4 7.4 %apply_renewed.6 = (bf16[8,1024,512]{2,1,0:T(8,128)(2,1)}, bf16[1024,512]{1,0:T(8,128)(2,1)}) custom-call(s32[4]{0:T(128)} %pad_add_fusion.pos, bf16[8,1024,512]{2,1,0:T(8,128)(2,1)} %q0.7, bf16[4,1024,512]{2,1,0:T(8,128)(2,1)} %collective-permute-done.7.q1, ...), custom_call_target="tpu_custom_call", output_to_operand_aliasing={{0}: (8, {})} | custom-call | flops 3221225472 | bytes 7340032 | tf_op jit(solution)/shard_map/apply_renewed/pallas_call | solution.py:117
  283.9 7.4 %apply_renewed.7 = (bf16[8,1024,512]{2,1,0:T(8,128)(2,1)}, bf16[1024,512]{1,0:T(8,128)(2,1)}) custom-call(s32[4]{0:T(128)} %pad_add_fusion.pos, bf16[8,1024,512]{2,1,0:T(8,128)(2,1)} %q0.7, bf16[4,1024,512]{2,1,0:T(8,128)(2,1)} %collective-permute-done.7.q1, ...), custom_call_target="tpu_custom_call", output_to_operand_aliasing={{0}: (6, {})} | custom-call | flops 3221225472 | bytes 7340032 | tf_op jit(solution)/shard_map/apply_renewed/pallas_call | solution.py:117
  (103 shorter events, 90.7 us)
Async XLA Ops:
  0.0 65.2 %collective-permute-start.8 = (bf16[8,1024,512]{2,1,0:T(8,128)(2,1)}, bf16[8,1024,512]{2,1,0:T(8,128)(2,1)}, u32[]{:S(2)}, u32[]{:S(2)}) collective-permute-start(bf16[8,1024,512]{2,1,0:T(8,128)(2,1)} %refs_0_.11), channel_id=1, source_target_pairs={{0,1},{1,0},{2,3},{3,2},{4,5},{5,4},{6,7},{7,6},{8,9},{9,8},{10,11... | collective-permute-start | bytes 25165832 | tf_op jit(solution)/shard_map/ppermute | solution.py:517
  0.5 68.0 %collective-permute-start.9 = (bf16[8,1024,512]{2,1,0:T(8,128)(2,1)}, bf16[8,1024,512]{2,1,0:T(8,128)(2,1)}, u32[]{:S(2)}, u32[]{:S(2)}) collective-permute-start(bf16[8,1024,512]{2,1,0:T(8,128)(2,1)} %refs_2_.9), channel_id=1, source_target_pairs={{0,1},{1,0},{2,3},{3,2},{4,5},{5,4},{6,7},{7,6},{8,9},{9,8},{10,11... | collective-permute-start | bytes 25165832 | tf_op jit(solution)/shard_map/ppermute | solution.py:517
  62.5 22.0 %collective-permute-start.20 = (bf16[4,3,128,256]{3,2,1,0:T(8,128)(2,1)}, bf16[4,3,128,256]{3,2,1,0:T(8,128)(2,1)}, u32[]{:S(2)}, u32[]{:S(2)}) collective-permute-start(bf16[4,3,128,256]{3,2,1,0:T(8,128)(2,1)} %get-tuple-element.67.refs_10_.refs_6_), channel_id=1, source_target_pairs={{0,16},{16,0},{1,17},{17,1},{2,18},{18,2},{3,19},{19,3},{4,20},{20... | collective-permute-start | bytes 2359304 | tf_op jit(solution)/shard_map/ppermute | solution.py:520
  65.2 18.8 %collective-permute-start.19 = (bf16[3,128,256]{2,1,0:T(8,128)(2,1)}, bf16[3,128,256]{2,1,0:T(8,128)(2,1)}, u32[]{:S(2)}, u32[]{:S(2)}) collective-permute-start(bf16[3,128,256]{2,1,0:T(8,128)(2,1)} %get-tuple-element.66), channel_id=1, source_target_pairs={{0,12},{2,14},{4,8},{6,10},{8,4},{10,6},{12,0},{14,2},{1,13},{3,15... | collective-permute-start | bytes 589832 | tf_op jit(solution)/shard_map/ppermute | solution.py:526
  87.8 28.9 %collective-permute-start.28 = (bf16[4,3,128,256]{3,2,1,0:T(8,128)(2,1)}, bf16[4,3,128,256]{3,2,1,0:T(8,128)(2,1)}, u32[]{:S(2)}, u32[]{:S(2)}) collective-permute-start(bf16[4,3,128,256]{3,2,1,0:T(8,128)(2,1)} %get-tuple-element.77.refs_8_.refs_6_), channel_id=1, source_target_pairs={{0,16},{16,0},{1,17},{17,1},{2,18},{18,2},{3,19},{19,3},{4,20},{20... | collective-permute-start | bytes 2359304 | tf_op jit(solution)/shard_map/ppermute | solution.py:520
  95.6 142.3 %collective-permute-start.7 = (bf16[4,1024,512]{2,1,0:T(8,128)(2,1)}, bf16[4,1024,512]{2,1,0:T(8,128)(2,1)}, u32[]{:S(2)}, u32[]{:S(2)}) collective-permute-start(bf16[4,1024,512]{2,1,0:T(8,128)(2,1)} %other_half.1), channel_id=1, source_target_pairs={{0,1},{1,0},{2,3},{3,2},{4,5},{5,4},{6,7},{7,6},{8,9},{9,8},{10,11... | collective-permute-start | bytes 12582920 | tf_op jit(solution)/shard_map/ppermute | solution.py:517
  95.6 19.6 %collective-permute-start.21 = (bf16[3,128,256]{2,1,0:T(8,128)(2,1)}, bf16[3,128,256]{2,1,0:T(8,128)(2,1)}, u32[]{:S(2)}, u32[]{:S(2)}) collective-permute-start(bf16[3,128,256]{2,1,0:T(8,128)(2,1)} %get-tuple-element.70), channel_id=1, source_target_pairs={{0,4},{2,6},{4,0},{6,2},{8,12},{10,14},{12,8},{14,10},{1,5},{3,7},... | collective-permute-start | bytes 589832 | tf_op jit(solution)/shard_map/ppermute | solution.py:526
  96.3 20.4 %collective-permute-start.22 = (bf16[3,128,256]{2,1,0:T(8,128)(2,1)}, bf16[3,128,256]{2,1,0:T(8,128)(2,1)}, u32[]{:S(2)}, u32[]{:S(2)}) collective-permute-start(bf16[3,128,256]{2,1,0:T(8,128)(2,1)} %get-tuple-element.71), channel_id=1, source_target_pairs={{0,8},{2,10},{4,12},{6,14},{8,0},{10,2},{12,4},{14,6},{1,9},{3,11}... | collective-permute-start | bytes 589832 | tf_op jit(solution)/shard_map/ppermute | solution.py:526
  97.5 19.2 %collective-permute-start.23 = (bf16[3,128,256]{2,1,0:T(8,128)(2,1)}, bf16[3,128,256]{2,1,0:T(8,128)(2,1)}, u32[]{:S(2)}, u32[]{:S(2)}) collective-permute-start(bf16[3,128,256]{2,1,0:T(8,128)(2,1)} %get-tuple-element.72), channel_id=1, source_target_pairs={{0,12},{2,14},{4,8},{6,10},{8,4},{10,6},{12,0},{14,2},{1,13},{3,15... | collective-permute-start | bytes 589832 | tf_op jit(solution)/shard_map/ppermute | solution.py:526
  115.2 19.4 %collective-permute-start.30 = (bf16[3,512,256]{2,1,0:T(8,128)(2,1)}, bf16[3,512,256]{2,1,0:T(8,128)(2,1)}, u32[]{:S(2)}, u32[]{:S(2)}) collective-permute-start(bf16[3,512,256]{2,1,0:T(8,128)(2,1)} %get-tuple-element.79), channel_id=1, source_target_pairs={{0,2},{2,0},{4,6},{6,4},{8,10},{10,8},{12,14},{14,12},{1,3},{3,1},... | collective-permute-start | bytes 2359304 | tf_op jit(solution)/shard_map/ppermute | solution.py:523
  116.7 19.1 %collective-permute-start.31 = (bf16[3,512,256]{2,1,0:T(8,128)(2,1)}, bf16[3,512,256]{2,1,0:T(8,128)(2,1)}, u32[]{:S(2)}, u32[]{:S(2)}) collective-permute-start(bf16[3,512,256]{2,1,0:T(8,128)(2,1)} %added.4.refs_4_), channel_id=1, source_target_pairs={{0,4},{2,6},{4,0},{6,2},{8,12},{10,14},{12,8},{14,10},{1,5},{3,7},... | collective-permute-start | bytes 2359304 | tf_op jit(solution)/shard_map/ppermute | solution.py:526
  119.5 19.9 %collective-permute-start.29 = (bf16[4,3,128,256]{3,2,1,0:T(8,128)(2,1)}, bf16[4,3,128,256]{3,2,1,0:T(8,128)(2,1)}, u32[]{:S(2)}, u32[]{:S(2)}) collective-permute-start(bf16[4,3,128,256]{3,2,1,0:T(8,128)(2,1)} %next_pieces.7.refs_8_.refs_6_), channel_id=1, source_target_pairs={{0,16},{16,0},{1,17},{17,1},{2,18},{18,2},{3,19},{19,3},{4,20},{20... | collective-permute-start | bytes 2359304 | tf_op jit(solution)/shard_map/ppermute | solution.py:520
  132.8 19.1 %collective-permute-start.33 = (bf16[3,512,256]{2,1,0:T(8,128)(2,1)}, bf16[3,512,256]{2,1,0:T(8,128)(2,1)}, u32[]{:S(2)}, u32[]{:S(2)}) collective-permute-start(bf16[3,512,256]{2,1,0:T(8,128)(2,1)} %get-tuple-element.82), channel_id=1, source_target_pairs={{0,2},{2,0},{4,6},{6,4},{8,10},{10,8},{12,14},{14,12},{1,3},{3,1},... | collective-permute-start | bytes 2359304 | tf_op jit(solution)/shard_map/ppermute | solution.py:523
  139.4 36.0 %collective-permute-start.32 = (bf16[3,512,256]{2,1,0:T(8,128)(2,1)}, bf16[3,512,256]{2,1,0:T(8,128)(2,1)}, u32[]{:S(2)}, u32[]{:S(2)}) collective-permute-start(bf16[3,512,256]{2,1,0:T(8,128)(2,1)} %added.5.refs_8_), channel_id=1, source_target_pairs={{0,8},{2,10},{4,12},{6,14},{8,0},{10,2},{12,4},{14,6},{1,9},{3,11}... | collective-permute-start | bytes 2359304 | tf_op jit(solution)/shard_map/ppermute | solution.py:526
  155.3 34.9 %collective-permute-start.35 = (bf16[3,512,256]{2,1,0:T(8,128)(2,1)}, bf16[3,512,256]{2,1,0:T(8,128)(2,1)}, u32[]{:S(2)}, u32[]{:S(2)}) collective-permute-start(bf16[3,512,256]{2,1,0:T(8,128)(2,1)} %added.6.refs_1_), channel_id=1, source_target_pairs={{0,4},{2,6},{4,0},{6,2},{8,12},{10,14},{12,8},{14,10},{1,5},{3,7},... | collective-permute-start | bytes 2359304 | tf_op jit(solution)/shard_map/ppermute | solution.py:526
  156.7 33.4 %collective-permute-start.34 = (bf16[3,512,256]{2,1,0:T(8,128)(2,1)}, bf16[3,512,256]{2,1,0:T(8,128)(2,1)}, u32[]{:S(2)}, u32[]{:S(2)}) collective-permute-start(bf16[3,512,256]{2,1,0:T(8,128)(2,1)} %get-tuple-element.83), channel_id=1, source_target_pairs={{0,2},{2,0},{4,6},{6,4},{8,10},{10,8},{12,14},{14,12},{1,3},{3,1},... | collective-permute-start | bytes 2359304 | tf_op jit(solution)/shard_map/ppermute | solution.py:523
  202.0 34.6 %collective-permute-start.37 = (bf16[3,512,256]{2,1,0:T(8,128)(2,1)}, bf16[3,512,256]{2,1,0:T(8,128)(2,1)}, u32[]{:S(2)}, u32[]{:S(2)}) collective-permute-start(bf16[3,512,256]{2,1,0:T(8,128)(2,1)} %renewed_block.1.held_ref), channel_id=1, source_target_pairs={{0,8},{2,10},{4,12},{6,14},{8,0},{10,2},{12,4},{14,6},{1,9},{3,11}... | collective-permute-start | bytes 2359304 | tf_op jit(solution)/shard_map/ppermute | solution.py:526
  202.0 35.9 %collective-permute-start.41 = (bf16[3,512,256]{2,1,0:T(8,128)(2,1)}, bf16[3,512,256]{2,1,0:T(8,128)(2,1)}, u32[]{:S(2)}, u32[]{:S(2)}) collective-permute-start(bf16[3,512,256]{2,1,0:T(8,128)(2,1)} %renewed_block.1.held_ref), channel_id=1, source_target_pairs={{0,2},{2,0},{4,6},{6,4},{8,10},{10,8},{12,14},{14,12},{1,3},{3,1},... | collective-permute-start | bytes 2359304 | tf_op jit(solution)/shard_map/ppermute | solution.py:523
  203.3 34.7 %collective-permute-start.42 = (bf16[3,512,256]{2,1,0:T(8,128)(2,1)}, bf16[3,512,256]{2,1,0:T(8,128)(2,1)}, u32[]{:S(2)}, u32[]{:S(2)}) collective-permute-start(bf16[3,512,256]{2,1,0:T(8,128)(2,1)} %renewed_block.1.held_ref), channel_id=1, source_target_pairs={{0,4},{2,6},{4,0},{6,2},{8,12},{10,14},{12,8},{14,10},{1,5},{3,7},... | collective-permute-start | bytes 2359304 | tf_op jit(solution)/shard_map/ppermute | solution.py:526
  236.6 19.2 %collective-permute-start.38 = (bf16[3,512,256]{2,1,0:T(8,128)(2,1)}, bf16[3,512,256]{2,1,0:T(8,128)(2,1)}, u32[]{:S(2)}, u32[]{:S(2)}) collective-permute-start(bf16[3,512,256]{2,1,0:T(8,128)(2,1)} %collective-permute-done.37.refs_1_.held_ref), channel_id=1, source_target_pairs={{0,4},{2,6},{4,0},{6,2},{8,12},{10,14},{12,8},{14,10},{1,5},{3,7},... | collective-permute-start | bytes 2359304 | tf_op jit(solution)/shard_map/ppermute | solution.py:526
  236.6 22.6 %collective-permute-start.40 = (bf16[3,512,256]{2,1,0:T(8,128)(2,1)}, bf16[3,512,256]{2,1,0:T(8,128)(2,1)}, u32[]{:S(2)}, u32[]{:S(2)}) collective-permute-start(bf16[3,512,256]{2,1,0:T(8,128)(2,1)} %collective-permute-done.37.refs_1_.held_ref), channel_id=1, source_target_pairs={{0,2},{2,0},{4,6},{6,4},{8,10},{10,8},{12,14},{14,12},{1,3},{3,1},... | collective-permute-start | bytes 2359304 | tf_op jit(solution)/shard_map/ppermute | solution.py:523
  245.0 21.3 %collective-permute-start.45 = (bf16[1024,512]{1,0:T(8,128)(2,1)}, bf16[1024,512]{1,0:T(8,128)(2,1)}, u32[]{:S(2)}, u32[]{:S(2)}) collective-permute-start(bf16[1024,512]{1,0:T(8,128)(2,1)} %get-tuple-element.91), channel_id=1, source_target_pairs={{0,1},{1,0},{2,3},{3,2},{4,5},{5,4},{6,7},{7,6},{8,9},{9,8},{10,11... | collective-permute-start | bytes 3145736 | tf_op jit(solution)/shard_map/ppermute | solution.py:517
  257.0 18.2 %collective-permute-start.44 = (bf16[3,512,256]{2,1,0:T(8,128)(2,1)}, bf16[3,512,256]{2,1,0:T(8,128)(2,1)}, u32[]{:S(2)}, u32[]{:S(2)}) collective-permute-start(bf16[3,512,256]{2,1,0:T(8,128)(2,1)} %get-tuple-element.89.refs_0_), channel_id=1, source_target_pairs={{0,4},{2,6},{4,0},{6,2},{8,12},{10,14},{12,8},{14,10},{1,5},{3,7},... | collective-permute-start | bytes 2359304 | tf_op jit(solution)/shard_map/ppermute | solution.py:526
  257.3 19.1 %collective-permute-start.39 = (bf16[3,512,256]{2,1,0:T(8,128)(2,1)}, bf16[3,512,256]{2,1,0:T(8,128)(2,1)}, u32[]{:S(2)}, u32[]{:S(2)}) collective-permute-start(bf16[3,512,256]{2,1,0:T(8,128)(2,1)} %collective-permute-done.38.refs_1_.held_ref), channel_id=1, source_target_pairs={{0,2},{2,0},{4,6},{6,4},{8,10},{10,8},{12,14},{14,12},{1,3},{3,1},... | collective-permute-start | bytes 2359304 | tf_op jit(solution)/shard_map/ppermute | solution.py:523
  (27 other events, 266.3 us)

commit v2 on v1

--- a/solution.py
+++ b/solution.py
@@ -287,10 +287,6 @@
 
         if last:
             own_copy().start()
-            squares = refs[n_in + 2 + cuts]
-            for m in range(3):
-                full = w[m].astype(F32)
-                squares[m : m + 1, :] = jnp.sum(full * full, axis=0, keepdims=True)
 
         @pl.loop(0, chunks)
         def _(c):
@@ -319,6 +315,11 @@
         def _(m):
             product(m, key[...], grads[m])
 
+        if last:
+            squares = refs[n_in + 2 + cuts]
+            for m in range(3):
+                full = w[m].astype(F32)
+                squares[m : m + 1, :] = jnp.sum(full * full, axis=0, keepdims=True)
         product(2, hidden[...], target[...])
         for m in range(3):
             for copy in out_copies(m):
@@ -433,9 +434,6 @@
         for copy in weights:
             copy.wait()
 
-        for n in range(len(blocks)):
-            late_in[n].wait()
-            late_out[n].start()
         for copy in loads:
             copy.wait()
 
@@ -451,6 +449,10 @@
             hidden = (gate * (0.5 * jnp.tanh(0.5 * gate) + 0.5) * up).astype(BF16)
             result[c * tile : (c + 1) * tile, :] = jnp.dot(hidden, w[2], preferred_element_type=F32).astype(BF16)
             stores[c].start()
+            if c == 0:
+                for n in range(len(blocks)):
+                    late_in[n].wait()
+                    late_out[n].start()
         for copy in stores + late_out:
             copy.wait()
 

time: 298 us -> 298 us (level)
  no operation moved by 1% of the time
where the time goes in v2:
time: 298 us; the launch traced here: 297 us
  Pallas kernels  131 us (44%)
  waiting for transfers between devices  112 us (38%)
  starting transfers between devices  52.1 us (17%)
    pallas_call x24, Pallas kernels, call(): pl.pallas_call(body, name=name, out_shape=out_shapes, grid_spec=pltpu.Pre...  131 us
    ppermute x19, waiting for transfers between devices, over_z(): return lax.ppermute(a, 'seq', [(i, i ^ 2 * j) for i in range(8)])  94.6 us
    ppermute x19, starting transfers between devices, over_z(): return lax.ppermute(a, 'seq', [(i, i ^ 2 * j) for i in range(8)])  27.2 us
    ppermute x13, starting transfers between devices, over_x(): return lax.ppermute(a, 'seq', [(i, i ^ 1) for i in range(8)])  16.1 us
    ppermute x11, waiting for transfers between devices, over_sub(): return lax.ppermute(a, 'sub', flip)  10.5 us
    ppermute x5, starting transfers between devices, over_groups(): return lax.ppermute(a, 'groups', flip)  6.59 us
  transfers between devices with their start and end apart: 48, of which 22 were waited for; matrix products, arithmetic and copies ran while one was open for 0% of the time, Pallas kernels for 43%

profile of v2, /device:TPU:0, one launch (start us, length us, event | category | flops | bytes accessed | tf_op | source)
XLA Modules:
  0.0 297.2 jit_solution(4611508899023120453)
XLA Ops:
  2.1 6.0 %collective-permute-done.refs_3_ = f32[8,32,512]{2,1,0:T(8,128)S(1)} collective-permute-done((f32[8,32,512]{2,1,0:T(8,128)}, f32[8,32,512]{2,1,0:T(8,128)S(1)}, u32[]{:S(2)}, u32[]{:S(2)}) %collective-permute-start) | collective-permute-done | bytes 524320 | tf_op jit(solution)/shard_map/ppermute | solution.py:519
  22.5 4.7 %collective-permute-start.5 = (bf16[3,64,256]{2,1,0:T(8,128)(2,1)}, bf16[3,64,256]{2,1,0:T(8,128)(2,1)}, u32[]{:S(2)}, u32[]{:S(2)}) collective-permute-start(bf16[3,64,256]{2,1,0:T(8,128)(2,1)} %get-tuple-element.54), channel_id=1, source_target_pairs={{0,12},{2,14},{4,8},{6,10},{8,4},{10,6},{12,0},{14,2},{1,13},{3,15... | collective-permute-start | bytes 294920 | tf_op jit(solution)/shard_map/ppermute | solution.py:528
  43.3 5.9 %collective-permute-done.12.refs_2_ = bf16[3,128,256]{2,1,0:T(8,128)(2,1)} collective-permute-done((bf16[3,128,256]{2,1,0:T(8,128)(2,1)}, bf16[3,128,256]{2,1,0:T(8,128)(2,1)}, u32[]{:S(2)}, u32[]{:S(2)}) %collective-permute-start.12) | collective-permute-done | bytes 196640 | tf_op jit(solution)/shard_map/ppermute | solution.py:528
  51.4 3.6 %token_rates.1 = (bf16[4,1024,128]{2,1,0:T(8,128)(2,1)}, bf16[4,1024,128]{2,1,0:T(8,128)(2,1)}) custom-call(s32[4]{0:T(128)} %pad_add_fusion.pos, s32[8,1024]{1,0:T(8,128)} %refs_0_.7, s32[8,1024]{1,0:T(8,128)} %collective-permute-done.10.refs_1_, bf16[4,3,64,256]{3,2,1,0:T(8,128)(2,1)} %get-tuple-element.56.rest_0_.refs_2_.refs_6_), custom_call_target="tpu_custom_call" | custom-call | tf_op jit(solution)/shard_map/token_rates/pallas_call | solution.py:117
  68.4 11.9 %gradients.4 = (f32[3,512,256]{2,1,0:T(8,128)}, bf16[3,128,256]{2,1,0:T(8,128)(2,1)}, bf16[3,128,256]{2,1,0:T(8,128)(2,1)}, bf16[3,128,256]{2,1,0:T(8,128)(2,1)}, bf16[3,128,256]{2,1,0:T(8,128)(2,1)}) custom-call(s32[4]{0:T(128)} %pad_add_fusion.pos, bf16[8,1024,512]{2,1,0:T(8,128)(2,1)} %refs_0_.11, bf16[8,1024,512]{2,1,0:T(8,128)(2,1)} %collective-permute-done.8.refs_1_, ...), custom_call_target="tpu_custom_call" | custom-call | flops 6442450944 | bytes 14680064 | tf_op jit(solution)/shard_map/gradients/pallas_call | solution.py:117
  84.5 3.3 %next_pieces.6 = (bf16[4,3,128,256]{3,2,1,0:T(8,128)(2,1)}, bf16[3,128,256]{2,1,0:T(8,128)(2,1)}, bf16[3,128,256]{2,1,0:T(8,128)(2,1)}, bf16[3,128,256]{2,1,0:T(8,128)(2,1)}, bf16[3,128,256]{2,1,0:T(8,128)(2,1)}) custom-call(s32[4]{0:T(128)} %pad_add_fusion.pos, bf16[3,128,256]{2,1,0:T(8,128)(2,1)} %get-tuple-element.63.refs_0_, ...), custom_call_target="tpu_custom_call" | custom-call | bytes 9000000 | tf_op jit(solution)/shard_map/next_pieces/pallas_call | solution.py:117
  88.3 7.3 %other_half.1 = bf16[4,1024,512]{2,1,0:T(8,128)(2,1)} custom-call(s32[4]{0:T(128)} %pad_add_fusion.pos, bf16[8,1024,512]{2,1,0:T(8,128)(2,1)} %q0.7, bf16[4,3,64,256]{3,2,1,0:T(8,128)(2,1)} %get-tuple-element.56.rest_0_.refs_2_.refs_6_), custom_call_target="tpu_custom_call" | custom-call | bytes 9000000 | tf_op jit(solution)/shard_map/other_half/pallas_call | solution.py:117
  100.1 11.8 %gradients.5 = (f32[3,512,256]{2,1,0:T(8,128)}, bf16[3,512,256]{2,1,0:T(8,128)(2,1)}) custom-call(s32[4]{0:T(128)} %pad_add_fusion.pos, bf16[8,1024,512]{2,1,0:T(8,128)(2,1)} %refs_0_.11, bf16[8,1024,512]{2,1,0:T(8,128)(2,1)} %collective-permute-done.8.refs_1_, bf16[8,1024,512]{2,1,0:T(8,128)(2,1)} %refs_2_.9, ...), custom_call_target="tpu_custom_call" | custom-call | flops 6442450944 | bytes 14680064 | tf_op jit(solution)/shard_map/gradients/pallas_call | solution.py:117
  111.9 3.3 %added.4.refs_4_ = bf16[3,512,256]{2,1,0:T(8,128)(2,1)} custom-call(s32[4]{0:T(128)} %pad_add_fusion.pos, f32[3,512,256]{2,1,0:T(8,128)} %get-tuple-element.68.refs_6_.keep_ref, bf16[3,128,256]{2,1,0:T(8,128)(2,1)} %collective-permute-done.24.refs_0_, bf16[3,128,256]{2,1,0:T(8,128)(2,1)} %collective-permute-done.25.refs_1_, ...), custom_call_target="tpu_custom_call" | custom-call | bytes 3000000 | tf_op jit(solution)/shard_map/added/pallas_call | solution.py:117
  121.0 11.8 %gradients.6 = (f32[3,512,256]{2,1,0:T(8,128)}, bf16[3,512,256]{2,1,0:T(8,128)(2,1)}) custom-call(s32[4]{0:T(128)} %pad_add_fusion.pos, bf16[8,1024,512]{2,1,0:T(8,128)(2,1)} %refs_0_.11, bf16[8,1024,512]{2,1,0:T(8,128)(2,1)} %collective-permute-done.8.refs_1_, bf16[8,1024,512]{2,1,0:T(8,128)(2,1)} %refs_2_.9, ...), custom_call_target="tpu_custom_call" | custom-call | flops 6442450944 | bytes 14680064 | tf_op jit(solution)/shard_map/gradients/pallas_call | solution.py:117
  135.8 3.6 %added.5.refs_8_ = bf16[3,512,256]{2,1,0:T(8,128)(2,1)} custom-call(s32[4]{0:T(128)} %pad_add_fusion.pos, f32[3,512,256]{2,1,0:T(8,128)} %get-tuple-element.78.refs_4_.keep_ref, bf16[3,512,256]{2,1,0:T(8,128)(2,1)} %collective-permute-done.30.refs_0_, bf16[3,512,256]{2,1,0:T(8,128)(2,1)} %collective-permute-done.31.refs_1_, ...), custom_call_target="tpu_custom_call" | custom-call | bytes 3000000 | tf_op jit(solution)/shard_map/added/pallas_call | solution.py:117
  139.4 12.5 %gradients.7 = (f32[3,512,256]{2,1,0:T(8,128)}, bf16[3,512,256]{2,1,0:T(8,128)(2,1)}, bf16[3,512,256]{2,1,0:T(8,128)(2,1)}, f32[8,512]{1,0:T(8,128)}) custom-call(s32[4]{0:T(128)} %pad_add_fusion.pos, bf16[8,1024,512]{2,1,0:T(8,128)(2,1)} %refs_0_.11, bf16[8,1024,512]{2,1,0:T(8,128)(2,1)} %collective-permute-done.8.refs_1_, bf16[8,1024,512]{2,1,0:T(8,128)(2,1)} %refs_2_.9, ...), custom_call_target="tpu_custom_call" | custom-call | flops 6442450944 | bytes 14680064 | tf_op jit(solution)/shard_map/gradients/pallas_call | solution.py:117
  157.5 17.9 %collective-permute-done.32.refs_0_ = bf16[3,512,256]{2,1,0:T(8,128)(2,1)} collective-permute-done((bf16[3,512,256]{2,1,0:T(8,128)(2,1)}, bf16[3,512,256]{2,1,0:T(8,128)(2,1)}, u32[]{:S(2)}, u32[]{:S(2)}) %collective-permute-start.32) | collective-permute-done | bytes 786464 | tf_op jit(solution)/shard_map/ppermute | solution.py:528
  175.4 3.6 %added.7.keep_ref = f32[3,512,256]{2,1,0:T(8,128)} custom-call(s32[4]{0:T(128)} %pad_add_fusion.pos, f32[3,512,256]{2,1,0:T(8,128)} %get-tuple-element.81.refs_1_.keep_ref, bf16[3,512,256]{2,1,0:T(8,128)(2,1)} %collective-permute-done.32.refs_0_, bf16[3,512,256]{2,1,0:T(8,128)(2,1)} %added.6.refs_1_), custom_call_target="tpu_custom_call" | custom-call | bytes 24000000 | tf_op jit(solution)/shard_map/added/pallas_call | solution.py:117
  179.0 11.1 %collective-permute-done.35.refs_1_ = bf16[3,512,256]{2,1,0:T(8,128)(2,1)} collective-permute-done((bf16[3,512,256]{2,1,0:T(8,128)(2,1)}, bf16[3,512,256]{2,1,0:T(8,128)(2,1)}, u32[]{:S(2)}, u32[]{:S(2)}) %collective-permute-start.35) | collective-permute-done | bytes 786464 | tf_op jit(solution)/shard_map/ppermute | solution.py:528
  190.2 4.2 %total_gradient.1 = (f32[3,512,256]{2,1,0:T(8,128)}, f32[8,128]{1,0:T(8,128)}) custom-call(s32[4]{0:T(128)} %pad_add_fusion.pos, f32[3,512,256]{2,1,0:T(8,128)} %added.7.keep_ref, bf16[3,512,256]{2,1,0:T(8,128)(2,1)} %collective-permute-done.34.refs_0_, bf16[3,512,256]{2,1,0:T(8,128)(2,1)} %collective-permute-done.35.refs_1_), custom_call_target="tpu_custom_call" | custom-call | tf_op jit(solution)/shard_map/total_gradient/pallas_call | solution.py:117
  198.2 3.8 %renewed_block.1.held_ref = bf16[3,512,256]{2,1,0:T(8,128)(2,1)} custom-call(s32[4]{0:T(128)} %pad_add_fusion.pos, f32[3,512,256]{2,1,0:T(8,128)} %get-tuple-element.84.g_ref, bf16[3,512,256]{2,1,0:T(8,128)(2,1)} %get-tuple-element.85.w_ref, f32[8,512]{1,0:T(8,128)} %get-tuple-element.86.sq_ref, f32[8,128]{1,0:T(8,128)} %get-tuple-element.87.sums_ref, ...), custom_call_target="tpu_custom_call" | custom-call | tf_op jit(solution)/shard_map/renewed_block/pallas_call | solution.py:117
  205.2 31.4 %collective-permute-done.37.refs_1_.held_ref = bf16[3,512,256]{2,1,0:T(8,128)(2,1)} collective-permute-done((bf16[3,512,256]{2,1,0:T(8,128)(2,1)}, bf16[3,512,256]{2,1,0:T(8,128)(2,1)}, u32[]{:S(2)}, u32[]{:S(2)}) %collective-permute-start.37) | collective-permute-done | bytes 786464 | tf_op jit(solution)/shard_map/ppermute | solution.py:528
  238.0 7.0 %apply_renewed.4 = (bf16[8,1024,512]{2,1,0:T(8,128)(2,1)}, bf16[1024,512]{1,0:T(8,128)(2,1)}) custom-call(s32[4]{0:T(128)} %pad_add_fusion.pos, bf16[8,1024,512]{2,1,0:T(8,128)(2,1)} %q0.7, bf16[4,1024,512]{2,1,0:T(8,128)(2,1)} %collective-permute-done.7.q1, bf16[3,512,256]{2,1,0:T(8,128)(2,1)} %renewed_block.1.held_ref, ...), custom_call_target="tpu_custom_call" | custom-call | flops 3221225472 | bytes 7340032 | tf_op jit(solution)/shard_map/apply_renewed/pallas_call | solution.py:117
  245.1 10.6 %collective-permute-done.38.refs_1_.held_ref = bf16[3,512,256]{2,1,0:T(8,128)(2,1)} collective-permute-done((bf16[3,512,256]{2,1,0:T(8,128)(2,1)}, bf16[3,512,256]{2,1,0:T(8,128)(2,1)}, u32[]{:S(2)}, u32[]{:S(2)}) %collective-permute-start.38) | collective-permute-done | bytes 786464 | tf_op jit(solution)/shard_map/ppermute | solution.py:528
  259.2 7.0 %apply_renewed.5 = (bf16[8,1024,512]{2,1,0:T(8,128)(2,1)}, bf16[1024,512]{1,0:T(8,128)(2,1)}) custom-call(s32[4]{0:T(128)} %pad_add_fusion.pos, bf16[8,1024,512]{2,1,0:T(8,128)(2,1)} %q0.7, bf16[4,1024,512]{2,1,0:T(8,128)(2,1)} %collective-permute-done.7.q1, ...), custom_call_target="tpu_custom_call", output_to_operand_aliasing={{0}: (6, {})} | custom-call | flops 3221225472 | bytes 7340032 | tf_op jit(solution)/shard_map/apply_renewed/pallas_call | solution.py:117
  266.4 8.9 %collective-permute-done.44.swapped_ref = bf16[3,512,256]{2,1,0:T(8,128)(2,1)} collective-permute-done((bf16[3,512,256]{2,1,0:T(8,128)(2,1)}, bf16[3,512,256]{2,1,0:T(8,128)(2,1)}, u32[]{:S(2)}, u32[]{:S(2)}) %collective-permute-start.44) | collective-permute-done | bytes 786464 | tf_op jit(solution)/shard_map/ppermute | solution.py:528
  276.4 7.2 %apply_renewed.6 = (bf16[8,1024,512]{2,1,0:T(8,128)(2,1)}, bf16[1024,512]{1,0:T(8,128)(2,1)}) custom-call(s32[4]{0:T(128)} %pad_add_fusion.pos, bf16[8,1024,512]{2,1,0:T(8,128)(2,1)} %q0.7, bf16[4,1024,512]{2,1,0:T(8,128)(2,1)} %collective-permute-done.7.q1, ...), custom_call_target="tpu_custom_call", output_to_operand_aliasing={{0}: (8, {})} | custom-call | flops 3221225472 | bytes 7340032 | tf_op jit(solution)/shard_map/apply_renewed/pallas_call | solution.py:117
  283.7 7.5 %apply_renewed.7 = (bf16[8,1024,512]{2,1,0:T(8,128)(2,1)}, bf16[1024,512]{1,0:T(8,128)(2,1)}) custom-call(s32[4]{0:T(128)} %pad_add_fusion.pos, bf16[8,1024,512]{2,1,0:T(8,128)(2,1)} %q0.7, bf16[4,1024,512]{2,1,0:T(8,128)(2,1)} %collective-permute-done.7.q1, ...), custom_call_target="tpu_custom_call", output_to_operand_aliasing={{0}: (6, {})} | custom-call | flops 3221225472 | bytes 7340032 | tf_op jit(solution)/shard_map/apply_renewed/pallas_call | solution.py:117
  (103 shorter events, 90.7 us)
Async XLA Ops:
  0.0 65.2 %collective-permute-start.8 = (bf16[8,1024,512]{2,1,0:T(8,128)(2,1)}, bf16[8,1024,512]{2,1,0:T(8,128)(2,1)}, u32[]{:S(2)}, u32[]{:S(2)}) collective-permute-start(bf16[8,1024,512]{2,1,0:T(8,128)(2,1)} %refs_0_.11), channel_id=1, source_target_pairs={{0,1},{1,0},{2,3},{3,2},{4,5},{5,4},{6,7},{7,6},{8,9},{9,8},{10,11... | collective-permute-start | bytes 25165832 | tf_op jit(solution)/shard_map/ppermute | solution.py:519
  0.5 68.0 %collective-permute-start.9 = (bf16[8,1024,512]{2,1,0:T(8,128)(2,1)}, bf16[8,1024,512]{2,1,0:T(8,128)(2,1)}, u32[]{:S(2)}, u32[]{:S(2)}) collective-permute-start(bf16[8,1024,512]{2,1,0:T(8,128)(2,1)} %refs_2_.9), channel_id=1, source_target_pairs={{0,1},{1,0},{2,3},{3,2},{4,5},{5,4},{6,7},{7,6},{8,9},{9,8},{10,11... | collective-permute-start | bytes 25165832 | tf_op jit(solution)/shard_map/ppermute | solution.py:519
  62.5 22.0 %collective-permute-start.20 = (bf16[4,3,128,256]{3,2,1,0:T(8,128)(2,1)}, bf16[4,3,128,256]{3,2,1,0:T(8,128)(2,1)}, u32[]{:S(2)}, u32[]{:S(2)}) collective-permute-start(bf16[4,3,128,256]{3,2,1,0:T(8,128)(2,1)} %get-tuple-element.67.refs_10_.refs_6_), channel_id=1, source_target_pairs={{0,16},{16,0},{1,17},{17,1},{2,18},{18,2},{3,19},{19,3},{4,20},{20... | collective-permute-start | bytes 2359304 | tf_op jit(solution)/shard_map/ppermute | solution.py:522
  65.2 18.8 %collective-permute-start.19 = (bf16[3,128,256]{2,1,0:T(8,128)(2,1)}, bf16[3,128,256]{2,1,0:T(8,128)(2,1)}, u32[]{:S(2)}, u32[]{:S(2)}) collective-permute-start(bf16[3,128,256]{2,1,0:T(8,128)(2,1)} %get-tuple-element.66), channel_id=1, source_target_pairs={{0,12},{2,14},{4,8},{6,10},{8,4},{10,6},{12,0},{14,2},{1,13},{3,15... | collective-permute-start | bytes 589832 | tf_op jit(solution)/shard_map/ppermute | solution.py:528
  87.8 28.9 %collective-permute-start.28 = (bf16[4,3,128,256]{3,2,1,0:T(8,128)(2,1)}, bf16[4,3,128,256]{3,2,1,0:T(8,128)(2,1)}, u32[]{:S(2)}, u32[]{:S(2)}) collective-permute-start(bf16[4,3,128,256]{3,2,1,0:T(8,128)(2,1)} %get-tuple-element.77.refs_8_.refs_6_), channel_id=1, source_target_pairs={{0,16},{16,0},{1,17},{17,1},{2,18},{18,2},{3,19},{19,3},{4,20},{20... | collective-permute-start | bytes 2359304 | tf_op jit(solution)/shard_map/ppermute | solution.py:522
  95.6 142.3 %collective-permute-start.7 = (bf16[4,1024,512]{2,1,0:T(8,128)(2,1)}, bf16[4,1024,512]{2,1,0:T(8,128)(2,1)}, u32[]{:S(2)}, u32[]{:S(2)}) collective-permute-start(bf16[4,1024,512]{2,1,0:T(8,128)(2,1)} %other_half.1), channel_id=1, source_target_pairs={{0,1},{1,0},{2,3},{3,2},{4,5},{5,4},{6,7},{7,6},{8,9},{9,8},{10,11... | collective-permute-start | bytes 12582920 | tf_op jit(solution)/shard_map/ppermute | solution.py:519
  95.6 19.6 %collective-permute-start.21 = (bf16[3,128,256]{2,1,0:T(8,128)(2,1)}, bf16[3,128,256]{2,1,0:T(8,128)(2,1)}, u32[]{:S(2)}, u32[]{:S(2)}) collective-permute-start(bf16[3,128,256]{2,1,0:T(8,128)(2,1)} %get-tuple-element.70), channel_id=1, source_target_pairs={{0,4},{2,6},{4,0},{6,2},{8,12},{10,14},{12,8},{14,10},{1,5},{3,7},... | collective-permute-start | bytes 589832 | tf_op jit(solution)/shard_map/ppermute | solution.py:528
  96.3 20.4 %collective-permute-start.22 = (bf16[3,128,256]{2,1,0:T(8,128)(2,1)}, bf16[3,128,256]{2,1,0:T(8,128)(2,1)}, u32[]{:S(2)}, u32[]{:S(2)}) collective-permute-start(bf16[3,128,256]{2,1,0:T(8,128)(2,1)} %get-tuple-element.71), channel_id=1, source_target_pairs={{0,8},{2,10},{4,12},{6,14},{8,0},{10,2},{12,4},{14,6},{1,9},{3,11}... | collective-permute-start | bytes 589832 | tf_op jit(solution)/shard_map/ppermute | solution.py:528
  97.5 19.2 %collective-permute-start.23 = (bf16[3,128,256]{2,1,0:T(8,128)(2,1)}, bf16[3,128,256]{2,1,0:T(8,128)(2,1)}, u32[]{:S(2)}, u32[]{:S(2)}) collective-permute-start(bf16[3,128,256]{2,1,0:T(8,128)(2,1)} %get-tuple-element.72), channel_id=1, source_target_pairs={{0,12},{2,14},{4,8},{6,10},{8,4},{10,6},{12,0},{14,2},{1,13},{3,15... | collective-permute-start | bytes 589832 | tf_op jit(solution)/shard_map/ppermute | solution.py:528
  115.2 19.4 %collective-permute-start.30 = (bf16[3,512,256]{2,1,0:T(8,128)(2,1)}, bf16[3,512,256]{2,1,0:T(8,128)(2,1)}, u32[]{:S(2)}, u32[]{:S(2)}) collective-permute-start(bf16[3,512,256]{2,1,0:T(8,128)(2,1)} %get-tuple-element.79), channel_id=1, source_target_pairs={{0,2},{2,0},{4,6},{6,4},{8,10},{10,8},{12,14},{14,12},{1,3},{3,1},... | collective-permute-start | bytes 2359304 | tf_op jit(solution)/shard_map/ppermute | solution.py:525
  116.7 19.1 %collective-permute-start.31 = (bf16[3,512,256]{2,1,0:T(8,128)(2,1)}, bf16[3,512,256]{2,1,0:T(8,128)(2,1)}, u32[]{:S(2)}, u32[]{:S(2)}) collective-permute-start(bf16[3,512,256]{2,1,0:T(8,128)(2,1)} %added.4.refs_4_), channel_id=1, source_target_pairs={{0,4},{2,6},{4,0},{6,2},{8,12},{10,14},{12,8},{14,10},{1,5},{3,7},... | collective-permute-start | bytes 2359304 | tf_op jit(solution)/shard_map/ppermute | solution.py:528
  119.5 19.9 %collective-permute-start.29 = (bf16[4,3,128,256]{3,2,1,0:T(8,128)(2,1)}, bf16[4,3,128,256]{3,2,1,0:T(8,128)(2,1)}, u32[]{:S(2)}, u32[]{:S(2)}) collective-permute-start(bf16[4,3,128,256]{3,2,1,0:T(8,128)(2,1)} %next_pieces.7.refs_8_.refs_6_), channel_id=1, source_target_pairs={{0,16},{16,0},{1,17},{17,1},{2,18},{18,2},{3,19},{19,3},{4,20},{20... | collective-permute-start | bytes 2359304 | tf_op jit(solution)/shard_map/ppermute | solution.py:522
  132.8 19.1 %collective-permute-start.33 = (bf16[3,512,256]{2,1,0:T(8,128)(2,1)}, bf16[3,512,256]{2,1,0:T(8,128)(2,1)}, u32[]{:S(2)}, u32[]{:S(2)}) collective-permute-start(bf16[3,512,256]{2,1,0:T(8,128)(2,1)} %get-tuple-element.82), channel_id=1, source_target_pairs={{0,2},{2,0},{4,6},{6,4},{8,10},{10,8},{12,14},{14,12},{1,3},{3,1},... | collective-permute-start | bytes 2359304 | tf_op jit(solution)/shard_map/ppermute | solution.py:525
  139.4 36.0 %collective-permute-start.32 = (bf16[3,512,256]{2,1,0:T(8,128)(2,1)}, bf16[3,512,256]{2,1,0:T(8,128)(2,1)}, u32[]{:S(2)}, u32[]{:S(2)}) collective-permute-start(bf16[3,512,256]{2,1,0:T(8,128)(2,1)} %added.5.refs_8_), channel_id=1, source_target_pairs={{0,8},{2,10},{4,12},{6,14},{8,0},{10,2},{12,4},{14,6},{1,9},{3,11}... | collective-permute-start | bytes 2359304 | tf_op jit(solution)/shard_map/ppermute | solution.py:528
  155.3 34.9 %collective-permute-start.35 = (bf16[3,512,256]{2,1,0:T(8,128)(2,1)}, bf16[3,512,256]{2,1,0:T(8,128)(2,1)}, u32[]{:S(2)}, u32[]{:S(2)}) collective-permute-start(bf16[3,512,256]{2,1,0:T(8,128)(2,1)} %added.6.refs_1_), channel_id=1, source_target_pairs={{0,4},{2,6},{4,0},{6,2},{8,12},{10,14},{12,8},{14,10},{1,5},{3,7},... | collective-permute-start | bytes 2359304 | tf_op jit(solution)/shard_map/ppermute | solution.py:528
  156.7 33.4 %collective-permute-start.34 = (bf16[3,512,256]{2,1,0:T(8,128)(2,1)}, bf16[3,512,256]{2,1,0:T(8,128)(2,1)}, u32[]{:S(2)}, u32[]{:S(2)}) collective-permute-start(bf16[3,512,256]{2,1,0:T(8,128)(2,1)} %get-tuple-element.83), channel_id=1, source_target_pairs={{0,2},{2,0},{4,6},{6,4},{8,10},{10,8},{12,14},{14,12},{1,3},{3,1},... | collective-permute-start | bytes 2359304 | tf_op jit(solution)/shard_map/ppermute | solution.py:525
  202.0 34.6 %collective-permute-start.37 = (bf16[3,512,256]{2,1,0:T(8,128)(2,1)}, bf16[3,512,256]{2,1,0:T(8,128)(2,1)}, u32[]{:S(2)}, u32[]{:S(2)}) collective-permute-start(bf16[3,512,256]{2,1,0:T(8,128)(2,1)} %renewed_block.1.held_ref), channel_id=1, source_target_pairs={{0,8},{2,10},{4,12},{6,14},{8,0},{10,2},{12,4},{14,6},{1,9},{3,11}... | collective-permute-start | bytes 2359304 | tf_op jit(solution)/shard_map/ppermute | solution.py:528
  202.0 35.9 %collective-permute-start.41 = (bf16[3,512,256]{2,1,0:T(8,128)(2,1)}, bf16[3,512,256]{2,1,0:T(8,128)(2,1)}, u32[]{:S(2)}, u32[]{:S(2)}) collective-permute-start(bf16[3,512,256]{2,1,0:T(8,128)(2,1)} %renewed_block.1.held_ref), channel_id=1, source_target_pairs={{0,2},{2,0},{4,6},{6,4},{8,10},{10,8},{12,14},{14,12},{1,3},{3,1},... | collective-permute-start | bytes 2359304 | tf_op jit(solution)/shard_map/ppermute | solution.py:525
  203.3 34.7 %collective-permute-start.42 = (bf16[3,512,256]{2,1,0:T(8,128)(2,1)}, bf16[3,512,256]{2,1,0:T(8,128)(2,1)}, u32[]{:S(2)}, u32[]{:S(2)}) collective-permute-start(bf16[3,512,256]{2,1,0:T(8,128)(2,1)} %renewed_block.1.held_ref), channel_id=1, source_target_pairs={{0,4},{2,6},{4,0},{6,2},{8,12},{10,14},{12,8},{14,10},{1,5},{3,7},... | collective-permute-start | bytes 2359304 | tf_op jit(solution)/shard_map/ppermute | solution.py:528
  236.6 19.2 %collective-permute-start.38 = (bf16[3,512,256]{2,1,0:T(8,128)(2,1)}, bf16[3,512,256]{2,1,0:T(8,128)(2,1)}, u32[]{:S(2)}, u32[]{:S(2)}) collective-permute-start(bf16[3,512,256]{2,1,0:T(8,128)(2,1)} %collective-permute-done.37.refs_1_.held_ref), channel_id=1, source_target_pairs={{0,4},{2,6},{4,0},{6,2},{8,12},{10,14},{12,8},{14,10},{1,5},{3,7},... | collective-permute-start | bytes 2359304 | tf_op jit(solution)/shard_map/ppermute | solution.py:528
  236.6 22.6 %collective-permute-start.40 = (bf16[3,512,256]{2,1,0:T(8,128)(2,1)}, bf16[3,512,256]{2,1,0:T(8,128)(2,1)}, u32[]{:S(2)}, u32[]{:S(2)}) collective-permute-start(bf16[3,512,256]{2,1,0:T(8,128)(2,1)} %collective-permute-done.37.refs_1_.held_ref), channel_id=1, source_target_pairs={{0,2},{2,0},{4,6},{6,4},{8,10},{10,8},{12,14},{14,12},{1,3},{3,1},... | collective-permute-start | bytes 2359304 | tf_op jit(solution)/shard_map/ppermute | solution.py:525
  245.0 21.3 %collective-permute-start.45 = (bf16[1024,512]{1,0:T(8,128)(2,1)}, bf16[1024,512]{1,0:T(8,128)(2,1)}, u32[]{:S(2)}, u32[]{:S(2)}) collective-permute-start(bf16[1024,512]{1,0:T(8,128)(2,1)} %get-tuple-element.91), channel_id=1, source_target_pairs={{0,1},{1,0},{2,3},{3,2},{4,5},{5,4},{6,7},{7,6},{8,9},{9,8},{10,11... | collective-permute-start | bytes 3145736 | tf_op jit(solution)/shard_map/ppermute | solution.py:519
  257.0 18.2 %collective-permute-start.44 = (bf16[3,512,256]{2,1,0:T(8,128)(2,1)}, bf16[3,512,256]{2,1,0:T(8,128)(2,1)}, u32[]{:S(2)}, u32[]{:S(2)}) collective-permute-start(bf16[3,512,256]{2,1,0:T(8,128)(2,1)} %get-tuple-element.89.refs_0_), channel_id=1, source_target_pairs={{0,4},{2,6},{4,0},{6,2},{8,12},{10,14},{12,8},{14,10},{1,5},{3,7},... | collective-permute-start | bytes 2359304 | tf_op jit(solution)/shard_map/ppermute | solution.py:528
  257.3 19.1 %collective-permute-start.39 = (bf16[3,512,256]{2,1,0:T(8,128)(2,1)}, bf16[3,512,256]{2,1,0:T(8,128)(2,1)}, u32[]{:S(2)}, u32[]{:S(2)}) collective-permute-start(bf16[3,512,256]{2,1,0:T(8,128)(2,1)} %collective-permute-done.38.refs_1_.held_ref), channel_id=1, source_target_pairs={{0,2},{2,0},{4,6},{6,4},{8,10},{10,8},{12,14},{14,12},{1,3},{3,1},... | collective-permute-start | bytes 2359304 | tf_op jit(solution)/shard_map/ppermute | solution.py:525
  (27 other events, 266.2 us)

commit v3 on v2

--- a/solution.py
+++ b/solution.py
@@ -348,20 +348,35 @@
 
 def added(positions, keep, received, after, dtype=BF16, microseconds=1, cuts=1):
     rows = keep.shape[1]
-
-    def body(pos, keep_ref, *refs):
+    n = len(received)
+
+    def body(pos, *refs):
+        sources, out = refs[: n + 1], refs[n + 1 + len(after)]
+        buffers, summed, sems = refs[-n - 3 : -2], refs[-2], refs[-1]
+        loads = [[pltpu.make_async_copy(a.at[m], b.at[m], sems.at[m, i]) for i, (a, b) in enumerate(zip(sources, buffers))] for m in range(3)]
+        stores = [pltpu.make_async_copy(summed.at[m], out.at[m], sems.at[m, n + 1]) for m in range(3)]
+        for copy in loads[0] + loads[1] + loads[2]:
+            copy.start()
         for m in range(3):
+            for copy in loads[m]:
+                copy.wait()
             for c in range(cuts):
                 at = pl.ds(c * (rows // cuts), rows // cuts)
-                total = keep_ref[m, at, :] + refs[c][m].astype(F32)
-                for ref in refs[cuts : len(received)]:
+                total = buffers[0][m, at, :] + buffers[1 + c][m].astype(F32)
+                for ref in buffers[1 + cuts :]:
                     total = total + ref[m, at, :].astype(F32)
-                refs[-1][m, at, :] = total.astype(dtype)
-
-    operands = (keep, *received)
+                summed[m, at, :] = total.astype(dtype)
+            stores[m].start()
+        for copy in stores:
+            copy.wait()
+
+    operands = (keep, *received, *after)
     shape = sds(keep.shape, dtype)
-    specs = [whole(a) for a in operands] + [anywhere()] * len(after)
-    return call(body, "added", positions, (1,), (*operands, *after), specs, shape, whole(shape), estimate=cost(microseconds))
+    return call(
+        body, "added", positions, (1,), operands, [anywhere()] * len(operands), shape, anywhere(),
+        [pltpu.VMEM(a.shape, a.dtype) for a in (keep, *received, shape)] + [pltpu.SemaphoreType.DMA((3, n + 2))],
+        estimate=cost(microseconds),
+    )
 
 
 def total_gradient(positions, keep, received):

time: 298 us -> 298 us (level)
  no operation moved by 1% of the time
where the time goes in v3:
time: 298 us; the launch traced here: 297 us
  Pallas kernels  130 us (44%)
  waiting for transfers between devices  113 us (38%)
  starting transfers between devices  51.6 us (17%)
    pallas_call x24, Pallas kernels, call(): pl.pallas_call(body, name=name, out_shape=out_shapes, grid_spec=pltpu.Pre...  130 us
    ppermute x19, waiting for transfers between devices, over_z(): return lax.ppermute(a, 'seq', [(i, i ^ 2 * j) for i in range(8)])  96.9 us
    ppermute x19, starting transfers between devices, over_z(): return lax.ppermute(a, 'seq', [(i, i ^ 2 * j) for i in range(8)])  27.3 us
    ppermute x13, starting transfers between devices, over_x(): return lax.ppermute(a, 'seq', [(i, i ^ 1) for i in range(8)])  15.5 us
    ppermute x11, waiting for transfers between devices, over_sub(): return lax.ppermute(a, 'sub', flip)  10.5 us
    ppermute x5, starting transfers between devices, over_groups(): return lax.ppermute(a, 'groups', flip)  6.59 us
  transfers between devices with their start and end apart: 48, of which 22 were waited for; matrix products, arithmetic and copies ran while one was open for 0% of the time, Pallas kernels for 43%

profile of v3, /device:TPU:0, one launch (start us, length us, event | category | flops | bytes accessed | tf_op | source)
XLA Modules:
  0.0 297.0 jit_solution(6107579350525064609)
XLA Ops:
  2.1 6.0 %collective-permute-done.refs_3_ = f32[8,32,512]{2,1,0:T(8,128)S(1)} collective-permute-done((f32[8,32,512]{2,1,0:T(8,128)}, f32[8,32,512]{2,1,0:T(8,128)S(1)}, u32[]{:S(2)}, u32[]{:S(2)}) %collective-permute-start) | collective-permute-done | bytes 524320 | tf_op jit(solution)/shard_map/ppermute | solution.py:534
  22.5 4.7 %collective-permute-start.5 = (bf16[3,64,256]{2,1,0:T(8,128)(2,1)}, bf16[3,64,256]{2,1,0:T(8,128)(2,1)}, u32[]{:S(2)}, u32[]{:S(2)}) collective-permute-start(bf16[3,64,256]{2,1,0:T(8,128)(2,1)} %get-tuple-element.54), channel_id=1, source_target_pairs={{0,12},{2,14},{4,8},{6,10},{8,4},{10,6},{12,0},{14,2},{1,13},{3,15... | collective-permute-start | bytes 294920 | tf_op jit(solution)/shard_map/ppermute | solution.py:543
  43.3 5.9 %collective-permute-done.12.refs_2_ = bf16[3,128,256]{2,1,0:T(8,128)(2,1)} collective-permute-done((bf16[3,128,256]{2,1,0:T(8,128)(2,1)}, bf16[3,128,256]{2,1,0:T(8,128)(2,1)}, u32[]{:S(2)}, u32[]{:S(2)}) %collective-permute-start.12) | collective-permute-done | bytes 196640 | tf_op jit(solution)/shard_map/ppermute | solution.py:543
  51.4 3.6 %token_rates.1 = (bf16[4,1024,128]{2,1,0:T(8,128)(2,1)}, bf16[4,1024,128]{2,1,0:T(8,128)(2,1)}) custom-call(s32[4]{0:T(128)} %pad_add_fusion.pos, s32[8,1024]{1,0:T(8,128)} %refs_0_.7, s32[8,1024]{1,0:T(8,128)} %collective-permute-done.10.refs_1_, bf16[4,3,64,256]{3,2,1,0:T(8,128)(2,1)} %get-tuple-element.56.rest_0_.refs_2_.refs_6_), custom_call_target="tpu_custom_call" | custom-call | tf_op jit(solution)/shard_map/token_rates/pallas_call | solution.py:117
  59.2 3.3 %next_pieces.5 = (bf16[4,3,128,256]{3,2,1,0:T(8,128)(2,1)}, bf16[3,128,256]{2,1,0:T(8,128)(2,1)}, bf16[3,128,256]{2,1,0:T(8,128)(2,1)}, bf16[3,128,256]{2,1,0:T(8,128)(2,1)}, bf16[3,128,256]{2,1,0:T(8,128)(2,1)}) custom-call(s32[4]{0:T(128)} %pad_add_fusion.pos, bf16[3,128,256]{2,1,0:T(8,128)(2,1)} %get-tuple-element.59.refs_0_, ...), custom_call_target="tpu_custom_call" | custom-call | bytes 9000000 | tf_op jit(solution)/shard_map/next_pieces/pallas_call | solution.py:117
  65.2 3.2 %collective-permute-start.19 = (bf16[3,128,256]{2,1,0:T(8,128)(2,1)}, bf16[3,128,256]{2,1,0:T(8,128)(2,1)}, u32[]{:S(2)}, u32[]{:S(2)}) collective-permute-start(bf16[3,128,256]{2,1,0:T(8,128)(2,1)} %get-tuple-element.66), channel_id=1, source_target_pairs={{0,12},{2,14},{4,8},{6,10},{8,4},{10,6},{12,0},{14,2},{1,13},{3,15... | collective-permute-start | bytes 589832 | tf_op jit(solution)/shard_map/ppermute | solution.py:543
  68.4 11.9 %gradients.4 = (f32[3,512,256]{2,1,0:T(8,128)}, bf16[3,128,256]{2,1,0:T(8,128)(2,1)}, bf16[3,128,256]{2,1,0:T(8,128)(2,1)}, bf16[3,128,256]{2,1,0:T(8,128)(2,1)}, bf16[3,128,256]{2,1,0:T(8,128)(2,1)}) custom-call(s32[4]{0:T(128)} %pad_add_fusion.pos, bf16[8,1024,512]{2,1,0:T(8,128)(2,1)} %refs_0_.11, bf16[8,1024,512]{2,1,0:T(8,128)(2,1)} %collective-permute-done.8.refs_1_, ...), custom_call_target="tpu_custom_call" | custom-call | flops 6442450944 | bytes 14680064 | tf_op jit(solution)/shard_map/gradients/pallas_call | solution.py:117
  84.5 3.3 %next_pieces.6 = (bf16[4,3,128,256]{3,2,1,0:T(8,128)(2,1)}, bf16[3,128,256]{2,1,0:T(8,128)(2,1)}, bf16[3,128,256]{2,1,0:T(8,128)(2,1)}, bf16[3,128,256]{2,1,0:T(8,128)(2,1)}, bf16[3,128,256]{2,1,0:T(8,128)(2,1)}) custom-call(s32[4]{0:T(128)} %pad_add_fusion.pos, bf16[3,128,256]{2,1,0:T(8,128)(2,1)} %get-tuple-element.63.refs_0_, ...), custom_call_target="tpu_custom_call" | custom-call | bytes 9000000 | tf_op jit(solution)/shard_map/next_pieces/pallas_call | solution.py:117
  88.3 7.3 %other_half.1 = bf16[4,1024,512]{2,1,0:T(8,128)(2,1)} custom-call(s32[4]{0:T(128)} %pad_add_fusion.pos, bf16[8,1024,512]{2,1,0:T(8,128)(2,1)} %q0.7, bf16[4,3,64,256]{3,2,1,0:T(8,128)(2,1)} %get-tuple-element.56.rest_0_.refs_2_.refs_6_), custom_call_target="tpu_custom_call" | custom-call | bytes 9000000 | tf_op jit(solution)/shard_map/other_half/pallas_call | solution.py:117
  100.1 11.8 %gradients.5 = (f32[3,512,256]{2,1,0:T(8,128)}, bf16[3,512,256]{2,1,0:T(8,128)(2,1)}) custom-call(s32[4]{0:T(128)} %pad_add_fusion.pos, bf16[8,1024,512]{2,1,0:T(8,128)(2,1)} %refs_0_.11, bf16[8,1024,512]{2,1,0:T(8,128)(2,1)} %collective-permute-done.8.refs_1_, bf16[8,1024,512]{2,1,0:T(8,128)(2,1)} %refs_2_.9, ...), custom_call_target="tpu_custom_call" | custom-call | flops 6442450944 | bytes 14680064 | tf_op jit(solution)/shard_map/gradients/pallas_call | solution.py:117
  120.9 11.8 %gradients.6 = (f32[3,512,256]{2,1,0:T(8,128)}, bf16[3,512,256]{2,1,0:T(8,128)(2,1)}) custom-call(s32[4]{0:T(128)} %pad_add_fusion.pos, bf16[8,1024,512]{2,1,0:T(8,128)(2,1)} %refs_0_.11, bf16[8,1024,512]{2,1,0:T(8,128)(2,1)} %collective-permute-done.8.refs_1_, bf16[8,1024,512]{2,1,0:T(8,128)(2,1)} %refs_2_.9, ...), custom_call_target="tpu_custom_call" | custom-call | flops 6442450944 | bytes 14680064 | tf_op jit(solution)/shard_map/gradients/pallas_call | solution.py:117
  135.6 3.4 %added.5.refs_8_ = bf16[3,512,256]{2,1,0:T(8,128)(2,1)} custom-call(s32[4]{0:T(128)} %pad_add_fusion.pos, f32[3,512,256]{2,1,0:T(8,128)} %get-tuple-element.78.refs_5_.refs_0_, bf16[3,512,256]{2,1,0:T(8,128)(2,1)} %collective-permute-done.30.refs_1_, bf16[3,512,256]{2,1,0:T(8,128)(2,1)} %collective-permute-done.31.refs_2_, ...), custom_call_target="tpu_custom_call" | custom-call | bytes 3000000 | tf_op jit(solution)/shard_map/added/pallas_call | solution.py:117
  139.1 12.5 %gradients.7 = (f32[3,512,256]{2,1,0:T(8,128)}, bf16[3,512,256]{2,1,0:T(8,128)(2,1)}, bf16[3,512,256]{2,1,0:T(8,128)(2,1)}, f32[8,512]{1,0:T(8,128)}) custom-call(s32[4]{0:T(128)} %pad_add_fusion.pos, bf16[8,1024,512]{2,1,0:T(8,128)(2,1)} %refs_0_.11, bf16[8,1024,512]{2,1,0:T(8,128)(2,1)} %collective-permute-done.8.refs_1_, bf16[8,1024,512]{2,1,0:T(8,128)(2,1)} %refs_2_.9, ...), custom_call_target="tpu_custom_call" | custom-call | flops 6442450944 | bytes 14680064 | tf_op jit(solution)/shard_map/gradients/pallas_call | solution.py:117
  157.3 17.8 %collective-permute-done.32.refs_1_ = bf16[3,512,256]{2,1,0:T(8,128)(2,1)} collective-permute-done((bf16[3,512,256]{2,1,0:T(8,128)(2,1)}, bf16[3,512,256]{2,1,0:T(8,128)(2,1)}, u32[]{:S(2)}, u32[]{:S(2)}) %collective-permute-start.32) | collective-permute-done | bytes 786464 | tf_op jit(solution)/shard_map/ppermute | solution.py:543
  178.3 11.4 %collective-permute-done.35.refs_1_ = bf16[3,512,256]{2,1,0:T(8,128)(2,1)} collective-permute-done((bf16[3,512,256]{2,1,0:T(8,128)(2,1)}, bf16[3,512,256]{2,1,0:T(8,128)(2,1)}, u32[]{:S(2)}, u32[]{:S(2)}) %collective-permute-start.35) | collective-permute-done | bytes 786464 | tf_op jit(solution)/shard_map/ppermute | solution.py:543
  189.7 4.2 %total_gradient.1 = (f32[3,512,256]{2,1,0:T(8,128)}, f32[8,128]{1,0:T(8,128)}) custom-call(s32[4]{0:T(128)} %pad_add_fusion.pos, f32[3,512,256]{2,1,0:T(8,128)} %added.7.keep_ref, bf16[3,512,256]{2,1,0:T(8,128)(2,1)} %collective-permute-done.34.refs_0_, bf16[3,512,256]{2,1,0:T(8,128)(2,1)} %collective-permute-done.35.refs_1_), custom_call_target="tpu_custom_call" | custom-call | tf_op jit(solution)/shard_map/total_gradient/pallas_call | solution.py:117
  197.8 3.8 %renewed_block.1.held_ref = bf16[3,512,256]{2,1,0:T(8,128)(2,1)} custom-call(s32[4]{0:T(128)} %pad_add_fusion.pos, f32[3,512,256]{2,1,0:T(8,128)} %get-tuple-element.84.g_ref, bf16[3,512,256]{2,1,0:T(8,128)(2,1)} %get-tuple-element.85.w_ref, f32[8,512]{1,0:T(8,128)} %get-tuple-element.86.sq_ref, f32[8,128]{1,0:T(8,128)} %get-tuple-element.87.sums_ref, ...), custom_call_target="tpu_custom_call" | custom-call | tf_op jit(solution)/shard_map/renewed_block/pallas_call | solution.py:117
  204.7 31.6 %collective-permute-done.37.refs_1_.held_ref = bf16[3,512,256]{2,1,0:T(8,128)(2,1)} collective-permute-done((bf16[3,512,256]{2,1,0:T(8,128)(2,1)}, bf16[3,512,256]{2,1,0:T(8,128)(2,1)}, u32[]{:S(2)}, u32[]{:S(2)}) %collective-permute-start.37) | collective-permute-done | bytes 786464 | tf_op jit(solution)/shard_map/ppermute | solution.py:543
  237.4 7.0 %apply_renewed.4 = (bf16[8,1024,512]{2,1,0:T(8,128)(2,1)}, bf16[1024,512]{1,0:T(8,128)(2,1)}) custom-call(s32[4]{0:T(128)} %pad_add_fusion.pos, bf16[8,1024,512]{2,1,0:T(8,128)(2,1)} %q0.7, bf16[4,1024,512]{2,1,0:T(8,128)(2,1)} %collective-permute-done.7.q1, bf16[3,512,256]{2,1,0:T(8,128)(2,1)} %renewed_block.1.held_ref, ...), custom_call_target="tpu_custom_call" | custom-call | flops 3221225472 | bytes 7340032 | tf_op jit(solution)/shard_map/apply_renewed/pallas_call | solution.py:117
  244.5 11.4 %collective-permute-done.38.refs_1_.held_ref = bf16[3,512,256]{2,1,0:T(8,128)(2,1)} collective-permute-done((bf16[3,512,256]{2,1,0:T(8,128)(2,1)}, bf16[3,512,256]{2,1,0:T(8,128)(2,1)}, u32[]{:S(2)}, u32[]{:S(2)}) %collective-permute-start.38) | collective-permute-done | bytes 786464 | tf_op jit(solution)/shard_map/ppermute | solution.py:543
  258.6 7.0 %apply_renewed.5 = (bf16[8,1024,512]{2,1,0:T(8,128)(2,1)}, bf16[1024,512]{1,0:T(8,128)(2,1)}) custom-call(s32[4]{0:T(128)} %pad_add_fusion.pos, bf16[8,1024,512]{2,1,0:T(8,128)(2,1)} %q0.7, bf16[4,1024,512]{2,1,0:T(8,128)(2,1)} %collective-permute-done.7.q1, ...), custom_call_target="tpu_custom_call", output_to_operand_aliasing={{0}: (6, {})} | custom-call | flops 3221225472 | bytes 7340032 | tf_op jit(solution)/shard_map/apply_renewed/pallas_call | solution.py:117
  265.7 10.1 %collective-permute-done.44.swapped_ref = bf16[3,512,256]{2,1,0:T(8,128)(2,1)} collective-permute-done((bf16[3,512,256]{2,1,0:T(8,128)(2,1)}, bf16[3,512,256]{2,1,0:T(8,128)(2,1)}, u32[]{:S(2)}, u32[]{:S(2)}) %collective-permute-start.44) | collective-permute-done | bytes 786464 | tf_op jit(solution)/shard_map/ppermute | solution.py:543
  276.2 7.2 %apply_renewed.6 = (bf16[8,1024,512]{2,1,0:T(8,128)(2,1)}, bf16[1024,512]{1,0:T(8,128)(2,1)}) custom-call(s32[4]{0:T(128)} %pad_add_fusion.pos, bf16[8,1024,512]{2,1,0:T(8,128)(2,1)} %q0.7, bf16[4,1024,512]{2,1,0:T(8,128)(2,1)} %collective-permute-done.7.q1, ...), custom_call_target="tpu_custom_call", output_to_operand_aliasing={{0}: (8, {})} | custom-call | flops 3221225472 | bytes 7340032 | tf_op jit(solution)/shard_map/apply_renewed/pallas_call | solution.py:117
  283.5 7.5 %apply_renewed.7 = (bf16[8,1024,512]{2,1,0:T(8,128)(2,1)}, bf16[1024,512]{1,0:T(8,128)(2,1)}) custom-call(s32[4]{0:T(128)} %pad_add_fusion.pos, bf16[8,1024,512]{2,1,0:T(8,128)(2,1)} %q0.7, bf16[4,1024,512]{2,1,0:T(8,128)(2,1)} %collective-permute-done.7.q1, ...), custom_call_target="tpu_custom_call", output_to_operand_aliasing={{0}: (6, {})} | custom-call | flops 3221225472 | bytes 7340032 | tf_op jit(solution)/shard_map/apply_renewed/pallas_call | solution.py:117
  (103 shorter events, 88.8 us)
Async XLA Ops:
  0.0 65.2 %collective-permute-start.8 = (bf16[8,1024,512]{2,1,0:T(8,128)(2,1)}, bf16[8,1024,512]{2,1,0:T(8,128)(2,1)}, u32[]{:S(2)}, u32[]{:S(2)}) collective-permute-start(bf16[8,1024,512]{2,1,0:T(8,128)(2,1)} %refs_0_.11), channel_id=1, source_target_pairs={{0,1},{1,0},{2,3},{3,2},{4,5},{5,4},{6,7},{7,6},{8,9},{9,8},{10,11... | collective-permute-start | bytes 25165832 | tf_op jit(solution)/shard_map/ppermute | solution.py:534
  0.5 68.0 %collective-permute-start.9 = (bf16[8,1024,512]{2,1,0:T(8,128)(2,1)}, bf16[8,1024,512]{2,1,0:T(8,128)(2,1)}, u32[]{:S(2)}, u32[]{:S(2)}) collective-permute-start(bf16[8,1024,512]{2,1,0:T(8,128)(2,1)} %refs_2_.9), channel_id=1, source_target_pairs={{0,1},{1,0},{2,3},{3,2},{4,5},{5,4},{6,7},{7,6},{8,9},{9,8},{10,11... | collective-permute-start | bytes 25165832 | tf_op jit(solution)/shard_map/ppermute | solution.py:534
  62.5 22.0 %collective-permute-start.20 = (bf16[4,3,128,256]{3,2,1,0:T(8,128)(2,1)}, bf16[4,3,128,256]{3,2,1,0:T(8,128)(2,1)}, u32[]{:S(2)}, u32[]{:S(2)}) collective-permute-start(bf16[4,3,128,256]{3,2,1,0:T(8,128)(2,1)} %get-tuple-element.67.refs_10_.refs_6_), channel_id=1, source_target_pairs={{0,16},{16,0},{1,17},{17,1},{2,18},{18,2},{3,19},{19,3},{4,20},{20... | collective-permute-start | bytes 2359304 | tf_op jit(solution)/shard_map/ppermute | solution.py:537
  65.2 18.8 %collective-permute-start.19 = (bf16[3,128,256]{2,1,0:T(8,128)(2,1)}, bf16[3,128,256]{2,1,0:T(8,128)(2,1)}, u32[]{:S(2)}, u32[]{:S(2)}) collective-permute-start(bf16[3,128,256]{2,1,0:T(8,128)(2,1)} %get-tuple-element.66), channel_id=1, source_target_pairs={{0,12},{2,14},{4,8},{6,10},{8,4},{10,6},{12,0},{14,2},{1,13},{3,15... | collective-permute-start | bytes 589832 | tf_op jit(solution)/shard_map/ppermute | solution.py:543
  87.8 28.7 %collective-permute-start.28 = (bf16[4,3,128,256]{3,2,1,0:T(8,128)(2,1)}, bf16[4,3,128,256]{3,2,1,0:T(8,128)(2,1)}, u32[]{:S(2)}, u32[]{:S(2)}) collective-permute-start(bf16[4,3,128,256]{3,2,1,0:T(8,128)(2,1)} %get-tuple-element.77.refs_8_.refs_6_), channel_id=1, source_target_pairs={{0,16},{16,0},{1,17},{17,1},{2,18},{18,2},{3,19},{19,3},{4,20},{20... | collective-permute-start | bytes 2359304 | tf_op jit(solution)/shard_map/ppermute | solution.py:537
  95.6 141.7 %collective-permute-start.7 = (bf16[4,1024,512]{2,1,0:T(8,128)(2,1)}, bf16[4,1024,512]{2,1,0:T(8,128)(2,1)}, u32[]{:S(2)}, u32[]{:S(2)}) collective-permute-start(bf16[4,1024,512]{2,1,0:T(8,128)(2,1)} %other_half.1), channel_id=1, source_target_pairs={{0,1},{1,0},{2,3},{3,2},{4,5},{5,4},{6,7},{7,6},{8,9},{9,8},{10,11... | collective-permute-start | bytes 12582920 | tf_op jit(solution)/shard_map/ppermute | solution.py:534
  95.6 19.4 %collective-permute-start.21 = (bf16[3,128,256]{2,1,0:T(8,128)(2,1)}, bf16[3,128,256]{2,1,0:T(8,128)(2,1)}, u32[]{:S(2)}, u32[]{:S(2)}) collective-permute-start(bf16[3,128,256]{2,1,0:T(8,128)(2,1)} %get-tuple-element.70), channel_id=1, source_target_pairs={{0,4},{2,6},{4,0},{6,2},{8,12},{10,14},{12,8},{14,10},{1,5},{3,7},... | collective-permute-start | bytes 589832 | tf_op jit(solution)/shard_map/ppermute | solution.py:543
  96.3 20.3 %collective-permute-start.22 = (bf16[3,128,256]{2,1,0:T(8,128)(2,1)}, bf16[3,128,256]{2,1,0:T(8,128)(2,1)}, u32[]{:S(2)}, u32[]{:S(2)}) collective-permute-start(bf16[3,128,256]{2,1,0:T(8,128)(2,1)} %get-tuple-element.71), channel_id=1, source_target_pairs={{0,8},{2,10},{4,12},{6,14},{8,0},{10,2},{12,4},{14,6},{1,9},{3,11}... | collective-permute-start | bytes 589832 | tf_op jit(solution)/shard_map/ppermute | solution.py:543
  97.5 19.0 %collective-permute-start.23 = (bf16[3,128,256]{2,1,0:T(8,128)(2,1)}, bf16[3,128,256]{2,1,0:T(8,128)(2,1)}, u32[]{:S(2)}, u32[]{:S(2)}) collective-permute-start(bf16[3,128,256]{2,1,0:T(8,128)(2,1)} %get-tuple-element.72), channel_id=1, source_target_pairs={{0,12},{2,14},{4,8},{6,10},{8,4},{10,6},{12,0},{14,2},{1,13},{3,15... | collective-permute-start | bytes 589832 | tf_op jit(solution)/shard_map/ppermute | solution.py:543
  115.0 19.4 %collective-permute-start.30 = (bf16[3,512,256]{2,1,0:T(8,128)(2,1)}, bf16[3,512,256]{2,1,0:T(8,128)(2,1)}, u32[]{:S(2)}, u32[]{:S(2)}) collective-permute-start(bf16[3,512,256]{2,1,0:T(8,128)(2,1)} %get-tuple-element.79), channel_id=1, source_target_pairs={{0,2},{2,0},{4,6},{6,4},{8,10},{10,8},{12,14},{14,12},{1,3},{3,1},... | collective-permute-start | bytes 2359304 | tf_op jit(solution)/shard_map/ppermute | solution.py:540
  116.6 19.1 %collective-permute-start.31 = (bf16[3,512,256]{2,1,0:T(8,128)(2,1)}, bf16[3,512,256]{2,1,0:T(8,128)(2,1)}, u32[]{:S(2)}, u32[]{:S(2)}) collective-permute-start(bf16[3,512,256]{2,1,0:T(8,128)(2,1)} %added.4.refs_4_), channel_id=1, source_target_pairs={{0,4},{2,6},{4,0},{6,2},{8,12},{10,14},{12,8},{14,10},{1,5},{3,7},... | collective-permute-start | bytes 2359304 | tf_op jit(solution)/shard_map/ppermute | solution.py:543
  119.4 19.7 %collective-permute-start.29 = (bf16[4,3,128,256]{3,2,1,0:T(8,128)(2,1)}, bf16[4,3,128,256]{3,2,1,0:T(8,128)(2,1)}, u32[]{:S(2)}, u32[]{:S(2)}) collective-permute-start(bf16[4,3,128,256]{3,2,1,0:T(8,128)(2,1)} %next_pieces.7.refs_8_.refs_6_), channel_id=1, source_target_pairs={{0,16},{16,0},{1,17},{17,1},{2,18},{18,2},{3,19},{19,3},{4,20},{20... | collective-permute-start | bytes 2359304 | tf_op jit(solution)/shard_map/ppermute | solution.py:537
  132.7 19.0 %collective-permute-start.33 = (bf16[3,512,256]{2,1,0:T(8,128)(2,1)}, bf16[3,512,256]{2,1,0:T(8,128)(2,1)}, u32[]{:S(2)}, u32[]{:S(2)}) collective-permute-start(bf16[3,512,256]{2,1,0:T(8,128)(2,1)} %get-tuple-element.82), channel_id=1, source_target_pairs={{0,2},{2,0},{4,6},{6,4},{8,10},{10,8},{12,14},{14,12},{1,3},{3,1},... | collective-permute-start | bytes 2359304 | tf_op jit(solution)/shard_map/ppermute | solution.py:540
  139.0 36.1 %collective-permute-start.32 = (bf16[3,512,256]{2,1,0:T(8,128)(2,1)}, bf16[3,512,256]{2,1,0:T(8,128)(2,1)}, u32[]{:S(2)}, u32[]{:S(2)}) collective-permute-start(bf16[3,512,256]{2,1,0:T(8,128)(2,1)} %added.5.refs_8_), channel_id=1, source_target_pairs={{0,8},{2,10},{4,12},{6,14},{8,0},{10,2},{12,4},{14,6},{1,9},{3,11}... | collective-permute-start | bytes 2359304 | tf_op jit(solution)/shard_map/ppermute | solution.py:543
  154.8 35.0 %collective-permute-start.35 = (bf16[3,512,256]{2,1,0:T(8,128)(2,1)}, bf16[3,512,256]{2,1,0:T(8,128)(2,1)}, u32[]{:S(2)}, u32[]{:S(2)}) collective-permute-start(bf16[3,512,256]{2,1,0:T(8,128)(2,1)} %added.6.refs_2_), channel_id=1, source_target_pairs={{0,4},{2,6},{4,0},{6,2},{8,12},{10,14},{12,8},{14,10},{1,5},{3,7},... | collective-permute-start | bytes 2359304 | tf_op jit(solution)/shard_map/ppermute | solution.py:543
  156.5 33.3 %collective-permute-start.34 = (bf16[3,512,256]{2,1,0:T(8,128)(2,1)}, bf16[3,512,256]{2,1,0:T(8,128)(2,1)}, u32[]{:S(2)}, u32[]{:S(2)}) collective-permute-start(bf16[3,512,256]{2,1,0:T(8,128)(2,1)} %get-tuple-element.83), channel_id=1, source_target_pairs={{0,2},{2,0},{4,6},{6,4},{8,10},{10,8},{12,14},{14,12},{1,3},{3,1},... | collective-permute-start | bytes 2359304 | tf_op jit(solution)/shard_map/ppermute | solution.py:540
  201.6 34.7 %collective-permute-start.37 = (bf16[3,512,256]{2,1,0:T(8,128)(2,1)}, bf16[3,512,256]{2,1,0:T(8,128)(2,1)}, u32[]{:S(2)}, u32[]{:S(2)}) collective-permute-start(bf16[3,512,256]{2,1,0:T(8,128)(2,1)} %renewed_block.1.held_ref), channel_id=1, source_target_pairs={{0,8},{2,10},{4,12},{6,14},{8,0},{10,2},{12,4},{14,6},{1,9},{3,11}... | collective-permute-start | bytes 2359304 | tf_op jit(solution)/shard_map/ppermute | solution.py:543
  201.6 35.8 %collective-permute-start.41 = (bf16[3,512,256]{2,1,0:T(8,128)(2,1)}, bf16[3,512,256]{2,1,0:T(8,128)(2,1)}, u32[]{:S(2)}, u32[]{:S(2)}) collective-permute-start(bf16[3,512,256]{2,1,0:T(8,128)(2,1)} %renewed_block.1.held_ref), channel_id=1, source_target_pairs={{0,2},{2,0},{4,6},{6,4},{8,10},{10,8},{12,14},{14,12},{1,3},{3,1},... | collective-permute-start | bytes 2359304 | tf_op jit(solution)/shard_map/ppermute | solution.py:540
  203.0 34.4 %collective-permute-start.42 = (bf16[3,512,256]{2,1,0:T(8,128)(2,1)}, bf16[3,512,256]{2,1,0:T(8,128)(2,1)}, u32[]{:S(2)}, u32[]{:S(2)}) collective-permute-start(bf16[3,512,256]{2,1,0:T(8,128)(2,1)} %renewed_block.1.held_ref), channel_id=1, source_target_pairs={{0,4},{2,6},{4,0},{6,2},{8,12},{10,14},{12,8},{14,10},{1,5},{3,7},... | collective-permute-start | bytes 2359304 | tf_op jit(solution)/shard_map/ppermute | solution.py:543
  236.3 19.6 %collective-permute-start.38 = (bf16[3,512,256]{2,1,0:T(8,128)(2,1)}, bf16[3,512,256]{2,1,0:T(8,128)(2,1)}, u32[]{:S(2)}, u32[]{:S(2)}) collective-permute-start(bf16[3,512,256]{2,1,0:T(8,128)(2,1)} %collective-permute-done.37.refs_1_.held_ref), channel_id=1, source_target_pairs={{0,4},{2,6},{4,0},{6,2},{8,12},{10,14},{12,8},{14,10},{1,5},{3,7},... | collective-permute-start | bytes 2359304 | tf_op jit(solution)/shard_map/ppermute | solution.py:543
  236.3 22.3 %collective-permute-start.40 = (bf16[3,512,256]{2,1,0:T(8,128)(2,1)}, bf16[3,512,256]{2,1,0:T(8,128)(2,1)}, u32[]{:S(2)}, u32[]{:S(2)}) collective-permute-start(bf16[3,512,256]{2,1,0:T(8,128)(2,1)} %collective-permute-done.37.refs_1_.held_ref), channel_id=1, source_target_pairs={{0,2},{2,0},{4,6},{6,4},{8,10},{10,8},{12,14},{14,12},{1,3},{3,1},... | collective-permute-start | bytes 2359304 | tf_op jit(solution)/shard_map/ppermute | solution.py:540
  244.4 21.3 %collective-permute-start.45 = (bf16[1024,512]{1,0:T(8,128)(2,1)}, bf16[1024,512]{1,0:T(8,128)(2,1)}, u32[]{:S(2)}, u32[]{:S(2)}) collective-permute-start(bf16[1024,512]{1,0:T(8,128)(2,1)} %get-tuple-element.91), channel_id=1, source_target_pairs={{0,1},{1,0},{2,3},{3,2},{4,5},{5,4},{6,7},{7,6},{8,9},{9,8},{10,11... | collective-permute-start | bytes 3145736 | tf_op jit(solution)/shard_map/ppermute | solution.py:534
  257.1 18.7 %collective-permute-start.44 = (bf16[3,512,256]{2,1,0:T(8,128)(2,1)}, bf16[3,512,256]{2,1,0:T(8,128)(2,1)}, u32[]{:S(2)}, u32[]{:S(2)}) collective-permute-start(bf16[3,512,256]{2,1,0:T(8,128)(2,1)} %get-tuple-element.89.refs_0_), channel_id=1, source_target_pairs={{0,4},{2,6},{4,0},{6,2},{8,12},{10,14},{12,8},{14,10},{1,5},{3,7},... | collective-permute-start | bytes 2359304 | tf_op jit(solution)/shard_map/ppermute | solution.py:543
  257.4 18.7 %collective-permute-start.39 = (bf16[3,512,256]{2,1,0:T(8,128)(2,1)}, bf16[3,512,256]{2,1,0:T(8,128)(2,1)}, u32[]{:S(2)}, u32[]{:S(2)}) collective-permute-start(bf16[3,512,256]{2,1,0:T(8,128)(2,1)} %collective-permute-done.38.refs_1_.held_ref), channel_id=1, source_target_pairs={{0,2},{2,0},{4,6},{6,4},{8,10},{10,8},{12,14},{14,12},{1,3},{3,1},... | collective-permute-start | bytes 2359304 | tf_op jit(solution)/shard_map/ppermute | solution.py:540
  (27 other events, 266.6 us)
